TPU v7x, 32 devices: a whole 2x2x4 slice. The times are simulated.
32 devices in a mesh: ctx: 8 (over z, x), tp: 4 (over y, core).
Axes of the slice: x: 2, y: 2, z: 4, core: 2. Of those that a mesh axis runs over, the one named last changes fastest.
Arguments:
- projected: bfloat16 [3, 4096, 8192], P(None, 'ctx', 'tp'), may hold values from -6 to 6
- short_filter: float32 [3, 3, 8192], P(None, None, 'tp'), may hold values from -3.5 to 3.5
- long_filter: bfloat16 [128, 8192], P(None, 'tp'), may hold values from -0.5 to 0.5
- skip_gain: float32 [8192], P('tp'), may hold values from -3 to 3
- out_weight: bfloat16 [8192, 8192], P('tp', 'ctx'), may hold values from -0.0625 to 0.0625
- out_grad: bfloat16 [4096, 8192], P('ctx'), may hold values from -6 to 6
- left_source: int32 [8], replicated, may hold values from -1 to 7, as said below
Outputs:
- mixed: bfloat16 [4096, 8192], P(('ctx', 'tp'))
- grad_projected: bfloat16 [3, 4096, 8192], P(None, 'ctx', 'tp')
- grad_long: float32 [128, 8192], P(None, 'tp')
- grad_short: float32 [3, 3, 8192], P(None, None, 'tp')
Inputs may be any that keep to these rules, and one draw needn't show every extreme that they name: left_source[b] is -1 where block b begins a contig, else another block; no block is named by two blocks, and following left_source from any block ends at -1 without repeating a block.
All inputs are finite; a program needn't handle non-finite values.
Results may differ from a plain program's by a relative error of at most 0.015.
Values may be sent and summed in bfloat16 or wider, within the bound.
A program may use at most 192 MiB of HBM per device.

v0:
```python
import math

import jax
import jax.numpy as jnp
from jax import lax
from jax.sharding import PartitionSpec as P

edge_depth = 8


def short_forward(extended, tap_weights, out_rows):
    summed = jnp.zeros((extended.shape[0], out_rows, extended.shape[2]), jnp.float32)
    for shift in range(tap_weights.shape[1]):
        piece = extended[:, edge_depth - shift : edge_depth - shift + out_rows].astype(jnp.float32)
        summed = summed + tap_weights[:, shift][:, None, :] * piece
    return summed


def depthwise(signal, kernel):
    channels = signal.shape[1]
    result = lax.conv_general_dilated(
        signal[None],
        kernel[:, None, :],
        (1,),
        "VALID",
        dimension_numbers=("NWC", "WIO", "NWC"),
        feature_group_count=channels,
        preferred_element_type=jnp.float32,
    )
    return result[0]


def causal_conv(extended, flipped_taps):
    return depthwise(extended[1:], flipped_taps)


def lag_sums(grad_conv, extended):
    return jnp.flip(depthwise(extended[1:], grad_conv), 0)


def select_slot(stacked, slot, live):
    picked = lax.dynamic_index_in_dim(stacked, slot, 0, keepdims=False)
    return jnp.where(live, picked, jnp.zeros_like(picked))


def on_device(projected, short_filter, long_filter, skip_gain, out_weight, out_grad, left_source):
    rows_here = projected.shape[1]
    filt_len = long_filter.shape[0]
    ctx_count = lax.axis_size("ctx")
    my_index = lax.axis_index("ctx")
    positions = jnp.arange(ctx_count, dtype=jnp.int32)
    source_raw = left_source[my_index]
    has_left = source_raw >= 0
    source = jnp.maximum(source_raw, 0)
    is_reader = left_source == my_index
    has_right = jnp.any(is_reader)
    reader = jnp.sum(jnp.where(is_reader, positions, 0))
    flipped_taps = jnp.flip(long_filter, 0)
    skip_row = skip_gain[None, :]
    act_rest = short_forward(projected, short_filter, rows_here - edge_depth)
    mixin_rest = (act_rest[1] * act_rest[2]).astype(jnp.bfloat16)
    raw_tail = projected[:, rows_here - edge_depth :]
    mixin_tail = mixin_rest[mixin_rest.shape[0] - filt_len :]
    slot_mark = ((positions == reader) & has_right).astype(jnp.bfloat16)
    sent_raw = slot_mark[:, None, None, None] * raw_tail[None]
    sent_mixin = slot_mark[:, None, None] * mixin_tail[None]
    got_raw, got_mixin = (
        lax.all_to_all(sent_raw, "ctx", split_axis=0, concat_axis=0, tiled=True),
        lax.all_to_all(sent_mixin, "ctx", split_axis=0, concat_axis=0, tiled=True),
    )
    left_raw = select_slot(got_raw, source, has_left)
    left_mixin = select_slot(got_mixin, source, has_left)
    streams_ext = jnp.concatenate([left_raw, projected], 1)
    act_head = short_forward(streams_ext[:, : 2 * edge_depth], short_filter, edge_depth)
    act = jnp.concatenate([act_head, act_rest], 1)
    mixin_head = (act_head[1] * act_head[2]).astype(jnp.bfloat16)
    mixin = jnp.concatenate([mixin_head, mixin_rest], 0)
    mixin_ext = jnp.concatenate([left_mixin, mixin], 0)
    conv = causal_conv(mixin_ext, flipped_taps)
    conv = conv + skip_row * mixin.astype(jnp.float32)
    gated = (act[0] * conv).astype(jnp.bfloat16)
    full_weight = lax.all_gather(out_weight, "ctx", axis=1, tiled=True)
    share_rows = rows_here // lax.axis_size("tp")
    gated_rows = lax.slice_in_dim(gated, 0, lax.axis_size("tp") * share_rows, axis=0)
    mixed = lax.psum_scatter(
        jnp.dot(gated_rows, full_weight, preferred_element_type=jnp.float32).astype(jnp.bfloat16),
        "tp",
        scatter_dimension=0,
        tiled=True,
    )
    back_grad = lax.dot_general(
        out_grad, full_weight, (((1,), (1,)), ((), ())), preferred_element_type=jnp.float32
    )
    grad_conv = (back_grad * act[0]).astype(jnp.bfloat16)
    grad_gate = back_grad * conv
    flipped = jnp.flip(grad_conv, 0)
    back_mark = ((positions == source) & has_left).astype(jnp.bfloat16)
    sent_head = back_mark[:, None, None] * grad_conv[None, :filt_len]
    got_head = lax.all_to_all(sent_head, "ctx", split_axis=0, concat_axis=0, tiled=True)
    right_head = select_slot(got_head, reader, has_right)
    flipped_ext = jnp.concatenate([jnp.flip(right_head, 0), flipped], 0)
    flipped_conv = causal_conv(flipped_ext, flipped_taps)
    grad_wide = grad_conv.astype(jnp.float32)
    grad_mixin = jnp.flip(flipped_conv, 0) + skip_row * grad_wide
    grad_act = jnp.stack([grad_gate, grad_mixin * act[2], grad_mixin * act[1]])
    wide_mark = back_mark.astype(jnp.float32)
    sent_rows = wide_mark[:, None, None, None] * grad_act[None, :, :edge_depth]
    got_rows = lax.all_to_all(
        sent_rows.astype(jnp.bfloat16), "ctx", split_axis=0, concat_axis=0, tiled=True
    ).astype(sent_rows.dtype)
    right_rows = select_slot(got_rows, reader, has_right)
    grad_act_ext = jnp.concatenate([grad_act, right_rows], 1)
    grad_streams = jnp.zeros(grad_act.shape, jnp.float32)
    for shift in range(short_filter.shape[1]):
        grad_streams = (
            grad_streams
            + short_filter[:, shift][:, None, :] * grad_act_ext[:, shift : shift + rows_here]
        )
    short_terms = jnp.stack(
        [
            jnp.sum(
                grad_act
                * streams_ext[:, edge_depth - shift : edge_depth - shift + rows_here].astype(
                    jnp.float32
                ),
                axis=1,
            )
            for shift in range(short_filter.shape[1])
        ],
        axis=1,
    )
    long_terms = lag_sums(grad_conv, mixin_ext)
    long_total, short_total = (
        lax.psum(long_terms.astype(jnp.bfloat16), "ctx").astype(jnp.float32),
        lax.psum(short_terms.astype(jnp.bfloat16), "ctx").astype(jnp.float32),
    )
    grad_scale = 1.0 / math.sqrt(rows_here * ctx_count)
    return (
        mixed,
        grad_streams.astype(jnp.bfloat16),
        long_total * grad_scale,
        short_total * grad_scale,
    )


def solution(mesh):
    placed = (
        P(None, "ctx", "tp"),
        P(None, None, "tp"),
        P(None, "tp"),
        P("tp"),
        P("tp", "ctx"),
        P("ctx", None),
        P(),
    )
    return jax.shard_map(
        on_device,
        mesh=mesh,
        in_specs=placed,
        out_specs=(
            P(("ctx", "tp"), None),
            P(None, "ctx", "tp"),
            P(None, "tp"),
            P(None, None, "tp"),
        ),
        check_vma=False,
    )
```

profile of v0, /device:TPU:0, one launch (start us, length us, event | category | flops | bytes accessed | tf_op | source)
XLA Modules:
  0.0 1070.3 jit_solution(15922003599213313523)
XLA Ops:
  7.2 0.0 slice-start.4
  7.2 0.0 all-gather.2.cloned.1.call-start
  7.2 0.7 all-gather.2.cloned.1.call-update
  7.9 0.6 compare_reduce_fusion
  8.6 0.6 fusion.28
  9.2 1.3 and_convert_fusion.1
  10.5 1.0 broadcast_multiply_fusion.2
  11.5 7.3 all-to-all-start
  18.8 0.1 fusion.32
  18.9 10.9 %multiply_add_fusion = f32[3,504,2048]{2,1,0:T(8,128)S(1)} fusion(bf16[3,512,2048]{2,1,0:T(8,128)(2,1)} %param.7, f32[3,2048]{1,0:T(4,128)S(1)} %get-tuple-element.21, f32[3,2048]{1,0:T(4,128)S(1)} %get-tuple-element.22, f32[3,2048]{1,0:T(4,128)S(1)} %bitcast.88), kind=kLoop, calls=%fused_computation.12 | loop fusion | flops 24772608 | bytes 31039488 | tf_op jit(solution)/shard_map/add | solution.py:15
  29.8 4.4 copy-done
  34.2 0.6 fusion.17
  34.9 2.4 broadcast_multiply_fusion.1
  37.3 10.4 all-to-all-done
  47.7 39.0 %all-to-all-start.1 = ((bf16[8,128,2048]{2,1,0:T(8,128)(2,1)}), bf16[8,128,2048]{2,1,0:T(8,128)(2,1)}, u32[]{:S(2)}, u32[]{:S(2)}) async-start(bf16[8,128,2048]{2,1,0:T(8,128)(2,1)} %broadcast_multiply_fusion.1), calls=%async_computation.1 | async-start | bytes 8388608 | tf_op jit(solution)/shard_map/all_to_all | solution.py:69
  86.7 0.6 dynamic_slice.18
  89.8 0.0 slice-start
  89.9 5.1 rev.19
  95.7 0.6 fusion.31
  96.2 5.5 fusion.36
  101.8 0.0 copy-start.5
  101.8 0.1 multiply_add_fusion.2
  101.9 0.0 copy-start.8
  102.0 113.5 %all-to-all-done.1 = bf16[8,128,2048]{2,1,0:T(8,128)(2,1)} async-done(((bf16[8,128,2048]{2,1,0:T(8,128)(2,1)}), bf16[8,128,2048]{2,1,0:T(8,128)(2,1)}, u32[]{:S(2)}, u32[]{:S(2)}) %all-to-all-start.1) | async-done | bytes 4194336 | tf_op jit(solution)/shard_map/all_to_all | solution.py:69
  215.5 1.1 select_bitcast_fusion.1
  216.6 2.2 fusion.22
  218.8 1.5 copy-done.2
  220.4 64.0 %fusion.19 = f32[1,512,2048]{2,0,1:T(1,128)} fusion(bf16[1,639,2048]{2,1,0:T(8,128)(2,1)S(1)} %fusion.22, bf16[128,1,2048]{2,0,1:T(8,128)(2,1)S(1)} %bitcast.87), kind=kOutput, calls=%fused_computation.43 | convolution fusion | flops 268435456 | bytes 7335936 | tf_op jit(solution)/shard_map/conv_general_dilated | solution.py:21
  284.4 419.0 %all-gather.2.cloned.1.call-done = bf16[2048,8192]{1,0:T(8,128)(2,1)} async-done(((bf16[2048,1024]{1,0:T(8,128)(2,1)}), bf16[2048,8192]{1,0:T(8,128)(2,1)}) %all-gather.2.cloned.1.call-update) | async-done | bytes 33554448 | tf_op jit(solution)/shard_map/all_gather | solution.py:82
  703.4 26.4 %multiply_bitcast_fusion = (f32[1,512,2048]{2,1,0:T(8,128)}, bf16[512,2048]{1,0:T(8,128)(2,1)S(1)}) fusion(f32[1,512,2048]{2,0,1:T(1,128)} %fusion.19, f32[2048]{0:T(1024)S(1)} %copy-done.18, bf16[504,2048]{1,0:T(8,128)(2,1)} %fusion.36, bf16[8,2048]{1,0:T(8,128)(2,1)S(1)} %fusion.27, f32[3,504,2048]{2,1,0:T(8,128)} %copy-done, ...), kind=kOutput, calls=%fused_computation.38 | convolution fusion | flops 17190354944 | bytes 67117056 | tf_op jit(solution)/shard_map/dot_general | solution.py:91
  729.9 2.4 broadcast_multiply_fusion
  732.3 4.6 all-to-all-start.2
  736.9 0.3 all-reduce.2.cloned.1.call-start
  737.1 0.0 copy-start.19
  737.2 55.8 %fusion.15 = bf16[1,128,2048]{2,0,1:T(2,128)(2,1)S(1)} fusion(bf16[512,1,2048]{2,0,1:T(8,128)(2,1)S(1)} %bitcast.84, bf16[1,639,2048]{2,1,0:T(8,128)(2,1)} %copy-done.2), kind=kOutput, calls=%fused_computation.34 | convolution fusion | flops 268435456 | bytes 5238784 | tf_op jit(solution)/shard_map/conv_general_dilated | solution.py:21
  793.0 0.3 copy.52
  793.3 5.2 rev.23
  798.4 0.0 all-reduce.2.cloned.1.call-update
  798.5 0.0 reduce-scatter.2.cloned.1.call-start
  798.5 30.5 %convolution_convert_fusion = bf16[512,8192]{1,0:T(8,128)(2,1)} fusion(bf16[2048,8192]{1,0:T(8,128)(2,1)} %all-gather.2.cloned.1.call-done, f32[1,512,2048]{2,0,1:T(1,128)} %fusion.19, f32[2048]{0:T(1024)S(1)} %copy-done.19, bf16[504,2048]{1,0:T(8,128)(2,1)} %fusion.36, bf16[8,2048]{1,0:T(8,128)(2,1)S(1)} %copy-done.16, f32[3,504,2048]{2,1,0:T(8,128)} %copy-done, ...), kind=kOutput, calls=%fused_computation.13 | convolution fusion | flops 17193500672 | bytes 60825600 | tf_op jit(solution)/shard_map/dot_general | solution.py:86
  829.1 20.4 %rev.21 = bf16[512,2048]{1,0:T(8,128)(2,1)} reverse(bf16[512,2048]{1,0:T(8,128)(2,1)S(1)} %get-tuple-element.17), dimensions={0} | reverse | bytes 4194304 | tf_op jit(solution)/shard_map/jit(_flip)/rev | solution.py:96
  849.5 0.0 reduce-scatter.2.cloned.1.call-update
  849.5 2.5 select_bitcast_fusion
  852.0 6.3 rev.20
  858.3 2.2 fusion.21
  860.6 63.5 %fusion.4 = f32[1,512,2048]{2,0,1:T(1,128)S(1)} fusion(bf16[1,639,2048]{2,1,0:T(8,128)(2,1)S(1)} %fusion.21, bf16[128,1,2048]{2,0,1:T(8,128)(2,1)} %bitcast.86), kind=kOutput, calls=%fused_computation.20 | convolution fusion | flops 268435456 | bytes 7335936 | tf_op jit(solution)/shard_map/conv_general_dilated | solution.py:21
  924.1 4.0 copy.51
  928.0 32.7 %rev.22 = f32[512,2048]{1,0:T(8,128)} reverse(f32[512,2048]{1,0:T(8,128)} %bitcast.83), dimensions={0} | reverse | bytes 8388608 | tf_op jit(solution)/shard_map/jit(_flip)/rev | solution.py:104
  960.8 7.1 fusion.9
  967.9 11.3 %pad_maximum_fusion.1 = f32[3,512,2048]{2,1,0:T(8,128)} fusion(f32[1,512,2048]{2,1,0:T(8,128)} %get-tuple-element.14, f32[1,512,2048]{2,1,0:T(8,128)S(1)} %get-tuple-element.13, f32[1,512,2048]{2,1,0:T(8,128)} %get-tuple-element.16), kind=kLoop, calls=%fused_computation.8 | loop fusion | flops 6291456 | bytes 25165824 | tf_op jit(solution)/shard_map/stack | solution.py:105
  979.2 0.9 slice.131
  980.1 1.1 multiply_convert_fusion.3
  981.2 5.7 all-to-all-start.3
  986.9 0.0 all-reduce.2.cloned.1.call-done
  986.9 0.0 slice-start.2
  986.9 2.3 convert_multiply_fusion
  989.2 17.5 %all-to-all-done.3 = bf16[8,3,8,2048]{3,2,1,0:T(8,128)(2,1)S(1)} async-done(((bf16[8,3,8,2048]{3,2,1,0:T(8,128)(2,1)}), bf16[8,3,8,2048]{3,2,1,0:T(8,128)(2,1)S(1)}, u32[]{:S(2)}, u32[]{:S(2)}) %all-to-all-start.3) | async-done | bytes 786464 | tf_op jit(solution)/shard_map/all_to_all | solution.py:108
  1006.7 0.6 select_bitcast_fusion.2
  1007.3 0.0 slice-start.3
  1007.4 0.0 copy-start.6
  1007.4 6.6 pad_maximum_fusion
  1014.1 13.3 %multiply_reduce_fusion.1 = (bf16[3,2048]{1,0:T(4,128)(2,1)S(1)}, bf16[3,2048]{1,0:T(4,128)(2,1)S(1)}, bf16[3,2048]{1,0:T(4,128)(2,1)S(1)}, bf16[3,512,2048]{2,1,0:T(8,128)(2,1)}) fusion(bf16[3,8,2048]{2,1,0:T(8,128)(2,1)S(1)} %copy-done.6, bf16[3,512,2048]{2,1,0:T(8,128)(2,1)S(1)} %bitcast.82, f32[1,512,2048]{2,1,0:T(8,128)} %get-tuple-element.14, ...), kind=kLoop, calls=%fused_computation.10 | loop fusion | flops 72333312 | bytes 50540544 | tf_op jit(solution)/shard_map/reduce_sum | solution.py:121
  1027.5 35.5 %psum.15 = bf16[3,3,2048]{2,0,1:T(4,128)(2,1)S(1)} all-reduce(bf16[3,3,2048]{2,0,1:T(4,128)(2,1)S(1)} %pad_maximum_fusion.9), channel_id=1, replica_groups=mesh['ctx'=8,'tp'=4] {'ctx'}, use_global_device_ids=true, to_apply=%region_7.8 | all-reduce | flops 18432 | bytes 73728 | tf_op jit(solution)/shard_map/psum | solution.py:135
  1063.1 0.7 copy.21
  (58 shorter events, 0.3 us)
Async XLA Ops:
  7.2 3.3 slice-start.4
  7.2 0.8 copy-start.22
  7.2 11.6 %copy-start.17 = (f32[3,3,2048]{2,1,0:T(4,128)S(1)}, f32[3,3,2048]{2,1,0:T(4,128)}, u32[]{:S(2)}) copy-start(f32[3,3,2048]{2,1,0:T(4,128)} %param.8) | copy-start | bytes 221188
  7.2 696.2 %all-gather.2.cloned.1.call-start = ((), (), s32[]{:S(2)}) async-start(), calls=%async_computation.5 | async-start | bytes 37748736 | tf_op jit(solution)/shard_map/all_gather | solution.py:82
  11.5 36.2 %all-to-all-start = ((bf16[8,3,8,2048]{3,2,1,0:T(8,128)(2,1)}), bf16[8,3,8,2048]{3,2,1,0:T(8,128)(2,1)S(1)}, u32[]{:S(2)}, u32[]{:S(2)}) async-start(bf16[8,3,8,2048]{3,2,1,0:T(8,128)(2,1)} %broadcast_multiply_fusion.2), calls=%async_computation | async-start | bytes 1572864 | tf_op jit(solution)/shard_map/all_to_all | solution.py:68
  18.9 82.9 %copy-start.9 = (f32[3,1,2048]{2,0,1:T(4,128)}, f32[3,1,2048]{2,0,1:T(4,128)S(1)}, u32[]{:S(2)}) copy-start(f32[3,1,2048]{2,0,1:T(4,128)S(1)} %copy.53) | copy-start | bytes 73732
  18.9 82.8 %copy-start.11 = (f32[3,2048]{1,0:T(4,128)}, f32[3,2048]{1,0:T(4,128)S(1)}, u32[]{:S(2)}) copy-start(f32[3,2048]{1,0:T(4,128)S(1)} %get-tuple-element.21) | copy-start | bytes 73732
  18.9 82.8 %copy-start.13 = (f32[3,2048]{1,0:T(4,128)}, f32[3,2048]{1,0:T(4,128)S(1)}, u32[]{:S(2)}) copy-start(f32[3,2048]{1,0:T(4,128)S(1)} %get-tuple-element.22) | copy-start | bytes 73732
  29.8 4.4 copy-start
  37.3 52.5 %copy-start.7 = (bf16[128,2048]{1,0:T(8,128)(2,1)S(1)}, bf16[128,2048]{1,0:T(8,128)(2,1)}, u32[]{:S(2)}) copy-start(bf16[128,2048]{1,0:T(8,128)(2,1)} %param.9) | copy-start | bytes 1572868
  47.7 167.8 %all-to-all-start.1 = ((bf16[8,128,2048]{2,1,0:T(8,128)(2,1)}), bf16[8,128,2048]{2,1,0:T(8,128)(2,1)}, u32[]{:S(2)}, u32[]{:S(2)}) async-start(bf16[8,128,2048]{2,1,0:T(8,128)(2,1)} %broadcast_multiply_fusion.1), calls=%async_computation.1 | async-start | bytes 8388608 | tf_op jit(solution)/shard_map/all_to_all | solution.py:69
  89.8 11.9 %slice-start = ((s8[6291456]{0:T(1024)(128)(4,1)}), s8[2097152]{0:T(1024)(128)(4,1)S(1)}, s32[]{:S(2)}) async-start(s8[6291456]{0:T(1024)(128)(4,1)} %bitcast.79), calls=%async_computation.8 | async-start | bytes 4194304
  96.2 5.5 slice-start.1
  101.8 117.0 %copy-start.5 = (bf16[3,8,2048]{2,1,0:T(8,128)(2,1)}, bf16[3,8,2048]{2,1,0:T(8,128)(2,1)S(1)}, u32[]{:S(2)}) copy-start(bf16[3,8,2048]{2,1,0:T(8,128)(2,1)S(1)} %select_bitcast_fusion.3) | copy-start | bytes 294916
  101.9 601.5 %copy-start.3 = (f32[3,8,2048]{2,1,0:T(8,128)}, f32[3,8,2048]{2,1,0:T(8,128)S(1)}, u32[]{:S(2)}) copy-start(f32[3,8,2048]{2,1,0:T(8,128)S(1)} %multiply_add_fusion.2) | copy-start | bytes 589828
  101.9 118.4 %copy-start.8 = (bf16[128,2048]{1,0:T(8,128)(2,1)S(1)}, bf16[128,2048]{1,0:T(8,128)(2,1)}, u32[]{:S(2)}) copy-start(bf16[128,2048]{1,0:T(8,128)(2,1)} %rev.19) | copy-start | bytes 1572868
  102.0 601.4 %copy-start.15 = (bf16[8,2048]{1,0:T(8,128)(2,1)}, bf16[8,2048]{1,0:T(8,128)(2,1)S(1)}, u32[]{:S(2)}) copy-start(bf16[8,2048]{1,0:T(8,128)(2,1)S(1)} %fusion.27) | copy-start | bytes 98308
  218.8 1.5 copy-start.2
  220.4 483.1 %copy-start.18 = (f32[2048]{0:T(1024)S(1)}, f32[2048]{0:T(1024)}, u32[]{:S(2)}) copy-start(f32[2048]{0:T(1024)} %param.10) | copy-start | bytes 24580
  284.4 445.5 %copy-start.21 = (bf16[8]{0:T(256)(128)(2,1)S(1)}, bf16[8]{0:T(256)(128)(2,1)}, u32[]{:S(2)}) copy-start(bf16[8]{0:T(256)(128)(2,1)} %get-tuple-element.12) | copy-start | bytes 52
  732.3 117.2 %all-to-all-start.2 = ((bf16[8,128,2048]{2,1,0:T(8,128)(2,1)}), bf16[8,128,2048]{2,1,0:T(8,128)(2,1)}, u32[]{:S(2)}, u32[]{:S(2)}) async-start(bf16[8,128,2048]{2,1,0:T(8,128)(2,1)} %broadcast_multiply_fusion), calls=%async_computation.3 | async-start | bytes 8388608 | tf_op jit(solution)/shard_map/all_to_all | solution.py:99
  736.9 250.1 %all-reduce.2.cloned.1.call-start = ((), (), s32[]{:S(2)}) async-start(), calls=%async_computation.7 | async-start | bytes 1048576 | tf_op jit(solution)/shard_map/psum | solution.py:134
  737.1 61.4 %copy-start.4 = (f32[3,8,2048]{2,1,0:T(8,128)S(1)}, f32[3,8,2048]{2,1,0:T(8,128)}, u32[]{:S(2)}) copy-start(f32[3,8,2048]{2,1,0:T(8,128)} %copy-done.3) | copy-start | bytes 589828
  737.1 61.4 %copy-start.16 = (bf16[8,2048]{1,0:T(8,128)(2,1)S(1)}, bf16[8,2048]{1,0:T(8,128)(2,1)}, u32[]{:S(2)}) copy-start(bf16[8,2048]{1,0:T(8,128)(2,1)} %copy-done.15) | copy-start | bytes 98308
  737.1 61.4 %copy-start.19 = (f32[2048]{0:T(1024)S(1)}, f32[2048]{0:T(1024)}, u32[]{:S(2)}) copy-start(f32[2048]{0:T(1024)} %param.10) | copy-start | bytes 24580
  798.5 265.3 %reduce-scatter.2.cloned.1.call-start = ((), (), s32[]{:S(2)}) async-start(), calls=%async_computation.6 | async-start | bytes 10485760 | tf_op jit(solution)/shard_map/reduce_scatter | solution.py:85
  967.9 11.3 %copy-start.1 = (f32[1,512,2048]{2,1,0:T(8,128)}, f32[1,512,2048]{2,1,0:T(8,128)S(1)}, u32[]{:S(2)}) copy-start(f32[1,512,2048]{2,1,0:T(8,128)S(1)} %get-tuple-element.13) | copy-start | bytes 12582916
  967.9 12.3 %copy-start.20 = (f32[8]{0:T(128)S(1)}, f32[8]{0:T(128)}, u32[]{:S(2)}) copy-start(f32[8]{0:T(128)} %get-tuple-element.11) | copy-start | bytes 100
  981.2 25.5 %all-to-all-start.3 = ((bf16[8,3,8,2048]{3,2,1,0:T(8,128)(2,1)}), bf16[8,3,8,2048]{3,2,1,0:T(8,128)(2,1)S(1)}, u32[]{:S(2)}, u32[]{:S(2)}) async-start(bf16[8,3,8,2048]{3,2,1,0:T(8,128)(2,1)} %multiply_convert_fusion.3), calls=%async_computation.4 | async-start | bytes 1572864 | tf_op jit(solution)/shard_map/all_to_all | solution.py:108
  986.9 27.1 %slice-start.2 = ((s8[6291456]{0:T(1024)(128)(4,1)}), s8[2097152]{0:T(1024)(128)(4,1)S(1)}, s32[]{:S(2)}) async-start(s8[6291456]{0:T(1024)(128)(4,1)} %bitcast.81), calls=%async_computation.10 | async-start | bytes 4194304
  1007.3 6.7 slice-start.3
  1007.4 6.7 copy-start.6
  1007.4 6.7 copy-start.10
  1007.4 6.7 copy-start.12
  1007.4 6.7 copy-start.14
Sparse Core Ops, SparseCore 0:
  9.6 693.7 all-gather.1
  798.6 78.3 all-reduce.1
  880.4 70.9 reduce-scatter.1
where the time goes:
time: 1070 us
  waiting for transfers between devices  561 us (52%)
  matrix products  240 us (22%)
  local copies, waits for them, and re-layouts  82.4 us (8%)
  other arithmetic  76.5 us (7%)
  starting transfers between devices  56.8 us (5%)
  blocking collectives  35.5 us (3%)
  between operations  17.6 us (2%)
    all_gather x1, waiting for transfers between devices, on_device(): full_weight = lax.all_gather(out_weight, 'ctx', axis=1, tiled=True)  419 us
    conv_general_dilated x3, matrix products, depthwise(): lax.conv_general_dilated(signal[None], kernel[:, None, :], (1,), 'VALID',...  183 us
    all_to_all x1, waiting for transfers between devices, on_device(): lax.all_to_all(sent_mixin, 'ctx', split_axis=0, concat_axis=0, tiled=True)  113 us
    all_to_all x1, starting transfers between devices, on_device(): lax.all_to_all(sent_mixin, 'ctx', split_axis=0, concat_axis=0, tiled=True)  39 us
    psum x1, blocking collectives, on_device(): lax.psum(short_terms.astype(jnp.bfloat16), 'ctx').astype(jnp.float32)  35.5 us
    rev x1, local copies, waits for them, and re-layouts, on_device(): grad_mixin = jnp.flip(flipped_conv, 0) + skip_row * grad_wide  32.7 us
    dot_general x1, matrix products, on_device(): jnp.dot(gated_rows, full_weight, preferred_element_type=jnp.float32)  30.5 us
    dot_general x1, matrix products, on_device(): lax.dot_general(out_grad, full_weight, (((1,), (1,)), ((), ())), preferre...  26.4 us
  transfers between devices with their start and end apart: 7, of which 4 were waited for; matrix products, arithmetic and copies ran while one was open for 34% of the time, Pallas kernels for 0%

commit v1 on v0

v1 whole, which is shorter than its diff:
```python
import math

import jax
import jax.numpy as jnp
from jax import lax
from jax.sharding import PartitionSpec as P

edge_depth = 8
chunk_count = 4
head_pad = 16


def short_forward(extended, tap_weights, out_rows):
    summed = jnp.zeros((extended.shape[0], out_rows, extended.shape[2]), jnp.float32)
    for shift in range(tap_weights.shape[1]):
        piece = extended[:, edge_depth - shift : edge_depth - shift + out_rows].astype(jnp.float32)
        summed = summed + tap_weights[:, shift][:, None, :] * piece
    return summed


def depthwise(signal, kernel):
    channels = signal.shape[1]
    result = lax.conv_general_dilated(
        signal[None],
        kernel[:, None, :],
        (1,),
        "VALID",
        dimension_numbers=("NWC", "WIO", "NWC"),
        feature_group_count=channels,
        preferred_element_type=jnp.float32,
    )
    return result[0]


def select_slot(stacked, slot, live):
    picked = lax.dynamic_index_in_dim(stacked, slot, 0, keepdims=False)
    return jnp.where(live, picked, jnp.zeros_like(picked))


def ring_order(count):
    return list(range(0, count, 2)) + list(range(1, count, 2))[::-1]


def on_device(projected, short_filter, long_filter, skip_gain, out_weight, out_grad, left_source):
    rows_here = projected.shape[1]
    channels = projected.shape[2]
    filt_len = long_filter.shape[0]
    taps = short_filter.shape[1]
    width = out_weight.shape[1]
    ctx_count = lax.axis_size("ctx")
    tp_count = lax.axis_size("tp")
    my_index = lax.axis_index("ctx")
    my_tp = lax.axis_index("tp")
    positions = jnp.arange(ctx_count, dtype=jnp.int32)
    source_raw = left_source[my_index]
    has_left = source_raw >= 0
    source = jnp.maximum(source_raw, 0)
    is_reader = left_source == my_index
    has_right = jnp.any(is_reader)
    reader = jnp.sum(jnp.where(is_reader, positions, 0))
    grad_scale = 1.0 / math.sqrt(rows_here * ctx_count)

    order = ring_order(ctx_count)
    order_table = jnp.array(order, jnp.int32)
    place_table = jnp.array([order.index(i) for i in range(ctx_count)], jnp.int32)
    place = place_table[my_index]
    ahead = [(order[i], order[(i + 1) % ctx_count]) for i in range(ctx_count)]
    behind = [(b, a) for a, b in ahead]
    half_ring = ctx_count // 2
    part = channels // chunk_count

    def owner_of(offset):
        return order_table[lax.rem(place + offset + ctx_count, ctx_count)]

    tail_rows = filt_len + edge_depth
    tail_act = short_forward(projected[:, rows_here - tail_rows :], short_filter, filt_len)
    mixin_tail = (tail_act[1] * tail_act[2]).astype(jnp.bfloat16)
    raw_tail = projected[:, rows_here - edge_depth :].reshape(3 * edge_depth, channels)
    got_tail = lax.all_gather(jnp.concatenate([mixin_tail, raw_tail], 0), "ctx", axis=0)
    left_tail = select_slot(got_tail, source, has_left)
    left_mixin = left_tail[:filt_len]
    left_raw = left_tail[filt_len:].reshape(3, edge_depth, channels)

    arrived = []
    for k in range(chunk_count):
        own = out_weight[k * part : (k + 1) * part]
        up, down = own, own
        if k >= 2:
            up, _ = lax.optimization_barrier((own, arrived[k - 2][-2][2]))
            down, _ = lax.optimization_barrier((own, arrived[k - 2][-1][2]))
        blocks = [(0, 0, own)]
        for step in range(1, half_ring):
            up = lax.ppermute(up, "ctx", ahead)
            down = lax.ppermute(down, "ctx", behind)
            blocks += [(-step, 0, up), (step, 0, down)]
        up = lax.ppermute(up[:, : width // 2], "ctx", ahead)
        down = lax.ppermute(down[:, width // 2 :], "ctx", behind)
        blocks += [(-half_ring, 0, up), (-half_ring, width // 2, down)]
        arrived.append(blocks)

    grad_pieces = [
        lax.dynamic_slice_in_dim(out_grad, owner_of(offset) * width + first, block.shape[1], 1)
        for offset, first, block in arrived[0]
    ]
    mixed_sums = [None] * len(grad_pieces)
    grad_streams_parts, long_parts, short_parts = [], [], []
    for k in range(chunk_count):
        cut = slice(k * part, (k + 1) * part)
        raw = projected[:, :, cut]
        short_taps = short_filter[:, :, cut]
        filt = long_filter[:, cut]
        flipped_taps = jnp.flip(filt, 0)
        skip_row = skip_gain[None, cut]
        act_rest = short_forward(raw, short_taps, rows_here - edge_depth)
        mixin_rest = (act_rest[1] * act_rest[2]).astype(jnp.bfloat16)
        head_rows = filt_len + head_pad
        conv_rest = depthwise(mixin_rest[head_pad + 1 - edge_depth :], flipped_taps)
        streams_ext = jnp.concatenate([left_raw[:, :, cut], raw], 1)
        act_head = short_forward(streams_ext[:, : 2 * edge_depth], short_taps, edge_depth)
        act = jnp.concatenate([act_head, act_rest], 1)
        mixin_head = (act_head[1] * act_head[2]).astype(jnp.bfloat16)
        mixin_ext = jnp.concatenate([left_mixin[:, cut], mixin_head, mixin_rest], 0)
        mixin = mixin_ext[filt_len:]
        conv_head = depthwise(mixin_ext[1 : filt_len + head_rows], flipped_taps)
        conv = jnp.concatenate([conv_head, conv_rest], 0)
        conv = conv + skip_row * mixin.astype(jnp.float32)
        gated = (act[0] * conv).astype(jnp.bfloat16)

        back_grad = None
        for j, (offset, first, block) in enumerate(arrived[k]):
            term = lax.dot_general(
                grad_pieces[j], block, (((1,), (1,)), ((), ())), preferred_element_type=jnp.float32
            )
            back_grad = term if back_grad is None else back_grad + term
            out_term = jnp.dot(gated, block, preferred_element_type=jnp.float32)
            mixed_sums[j] = out_term if k == 0 else mixed_sums[j] + out_term

        grad_conv = (back_grad * act[0]).astype(jnp.bfloat16)
        grad_gate = back_grad * conv
        got_head = lax.all_gather(grad_conv[:filt_len], "ctx", axis=0)
        right_head = select_slot(got_head, reader, has_right)
        mid_rows = rows_here - filt_len
        gm_rest = depthwise(grad_conv[: rows_here - 1], filt)
        gm_tail = depthwise(
            jnp.concatenate([grad_conv[mid_rows:], right_head], 0)[: 2 * filt_len - 1], filt
        )
        grad_mixin = jnp.concatenate([gm_rest, gm_tail], 0)
        grad_mixin = grad_mixin + skip_row * grad_conv.astype(jnp.float32)
        grad_act = jnp.stack([grad_gate, grad_mixin * act[2], grad_mixin * act[1]])
        got_rows = lax.all_gather(
            grad_act[:, :edge_depth].astype(jnp.bfloat16).reshape(3 * edge_depth, part), "ctx", axis=0
        )
        right_rows = select_slot(got_rows, reader, has_right).reshape(3, edge_depth, part)
        grad_act_ext = jnp.concatenate([grad_act, right_rows.astype(jnp.float32)], 1)
        grad_streams = jnp.zeros(grad_act.shape, jnp.float32)
        for shift in range(taps):
            grad_streams = (
                grad_streams
                + short_taps[:, shift][:, None, :] * grad_act_ext[:, shift : shift + rows_here]
            )
        grad_streams_parts.append(grad_streams.astype(jnp.bfloat16))
        short_terms = jnp.stack(
            [
                jnp.sum(
                    grad_act
                    * streams_ext[:, edge_depth - shift : edge_depth - shift + rows_here].astype(
                        jnp.float32
                    ),
                    axis=1,
                )
                for shift in range(taps)
            ],
            axis=1,
        )
        long_terms = depthwise(mixin_ext[1:], grad_conv)
        both = jnp.concatenate(
            [long_terms.astype(jnp.bfloat16), short_terms.reshape(3 * taps, part).astype(jnp.bfloat16)], 0
        )
        total = lax.psum(both, "ctx").astype(jnp.float32) * grad_scale
        long_parts.append(jnp.flip(total[:filt_len], 0))
        short_parts.append(total[filt_len:].reshape(3, taps, part))

    share = rows_here // tp_count
    mixed = jnp.zeros((share, width * ctx_count), jnp.bfloat16)
    for j, (offset, first, block) in enumerate(arrived[0]):
        piece = mixed_sums[j].astype(jnp.bfloat16).reshape(tp_count, share, block.shape[1])
        bit = 1
        while bit < tp_count:
            pairs = piece.reshape(piece.shape[0] // 2, 2, share, block.shape[1])
            mine = lax.rem(my_tp // bit, 2)
            kept = lax.dynamic_index_in_dim(pairs, mine, 1, keepdims=False)
            sent = lax.dynamic_index_in_dim(pairs, 1 - mine, 1, keepdims=False)
            got = lax.ppermute(sent, "tp", [(i, i ^ bit) for i in range(tp_count)])
            piece = (kept.astype(jnp.float32) + got.astype(jnp.float32)).astype(jnp.bfloat16)
            bit *= 2
        mixed = lax.dynamic_update_slice_in_dim(
            mixed, piece[0], owner_of(offset) * width + first, 1
        )
    return (
        mixed,
        jnp.concatenate(grad_streams_parts, 2),
        jnp.concatenate(long_parts, 1),
        jnp.concatenate(short_parts, 2),
    )


def solution(mesh):
    placed = (
        P(None, "ctx", "tp"),
        P(None, None, "tp"),
        P(None, "tp"),
        P("tp"),
        P("tp", "ctx"),
        P("ctx", None),
        P(),
    )
    return jax.shard_map(
        on_device,
        mesh=mesh,
        in_specs=placed,
        out_specs=(
            P(("ctx", "tp"), None),
            P(None, "ctx", "tp"),
            P(None, "tp"),
            P(None, None, "tp"),
        ),
        check_vma=False,
    )
```

time: 1070 us -> 1010 us (0.944)
  waiting for transfers between devices: 561 us -> 330 us
  blocking collectives: 35.5 us -> 122 us
  matrix products: 240 us -> 292 us
  other arithmetic: 76.5 us -> 103 us
  between operations: 17.6 us -> 31.6 us
    all_gather x1 -> x5, waiting for transfers between devices: 419 us -> 75 us  [the longest x4 75 us: on_device(): got_head = lax.all_gather(grad_conv[:filt_len], 'ctx', axis=0)]
    ppermute x0 -> x50, waiting for transfers between devices: none -> 221 us  [the longest x12 155 us: on_device(): down = lax.ppermute(down, 'ctx', behind)]
    all_to_all x4 -> x0, waiting for transfers between devices: 141 us -> none  [the longest x1 113 us: on_device(): lax.all_to_all(sent_mixin, 'ctx', split_axis=0, concat_axis=0, tiled=True)]
    all_gather x0 -> x4, blocking collectives: none -> 122 us  [on_device(): lax.all_gather(grad_act[:, :edge_depth].astype(jnp.bfloat16).reshape(3 *...]
    rev x5 -> x8, local copies, waits for them, and re-layouts: 69.8 us -> 7.32 us  [the longest x4 5.46 us: on_device(): long_parts.append(jnp.flip(total[:filt_len], 0))]
    all_to_all x4 -> x0, starting transfers between devices: 56.5 us -> none  [the longest x1 39 us: on_device(): lax.all_to_all(sent_mixin, 'ctx', split_axis=0, concat_axis=0, tiled=True)]
    dot_general x2 -> x72, matrix products: 56.9 us -> 107 us  [the longest x36 66 us: on_device(): lax.dot_general(grad_pieces[j], block, (((1,), (1,)), ((), ())), preferre...]
    ppermute x0 -> x50, starting transfers between devices: none -> 47.5 us  [the longest x12 23.7 us: on_device(): up = lax.ppermute(up, 'ctx', ahead)]
  transfers between devices with their start and end apart: 7 -> 56, of which waited for: 4 -> 22; matrix products, arithmetic and copies ran while one was open for 34% -> 36% of each run, Pallas kernels for 0% -> 0%
where the time goes in v1:
time: 1010 us; the launch traced here: 1000 us
  waiting for transfers between devices  330 us (33%)
  matrix products  292 us (29%)
  blocking collectives  122 us (12%)
  other arithmetic  103 us (10%)
  local copies, waits for them, and re-layouts  73.7 us (7%)
  starting transfers between devices  48.4 us (5%)
  between operations  31.6 us (3%)
    conv_general_dilated x20, matrix products, depthwise(): lax.conv_general_dilated(signal[None], kernel[:, None, :], (1,), 'VALID',...  185 us
    ppermute x12, waiting for transfers between devices, on_device(): down = lax.ppermute(down, 'ctx', behind)  155 us
    all_gather x4, blocking collectives, on_device(): lax.all_gather(grad_act[:, :edge_depth].astype(jnp.bfloat16).reshape(3 *...  122 us
    all_gather x4, waiting for transfers between devices, on_device(): got_head = lax.all_gather(grad_conv[:filt_len], 'ctx', axis=0)  75 us
    dot_general x36, matrix products, on_device(): lax.dot_general(grad_pieces[j], block, (((1,), (1,)), ((), ())), preferre...  66 us
    dot_general x36, matrix products, on_device(): out_term = jnp.dot(gated, block, preferred_element_type=jnp.float32)  41 us
    psum x1, waiting for transfers between devices, on_device(): total = lax.psum(both, 'ctx').astype(jnp.float32) * grad_scale  33.9 us
    unnamed x539, local copies, waits for them, and re-layouts  32.2 us
  transfers between devices with their start and end apart: 56, of which 22 were waited for; matrix products, arithmetic and copies ran while one was open for 36% of the time, Pallas kernels for 0%

profile of v1, /device:TPU:0, one launch (start us, length us, event | category | flops | bytes accessed | tf_op | source)
XLA Modules:
  0.0 1002.2 jit_solution(6693430505747887485)
XLA Ops:
  7.2 4.5 fusion.304
  28.2 9.2 multiply_add_fusion.1
  41.7 3.4 fusion.158
  45.1 3.3 fusion.162
  50.3 3.5 fusion.164
  62.2 11.7 %fusion.118 = f32[1,368,512]{2,0,1:T(1,128)S(1)} fusion(bf16[1,504,512]{2,1,0:T(8,128)(2,1)S(1)} %copy-done.205, bf16[128,1,512]{2,0,1:T(8,128)(2,1)S(1)} %bitcast.621), kind=kOutput, calls=%fused_computation.234 | convolution fusion | flops 48234496 | bytes 1400832 | tf_op jit(solution)/shard_map/conv_general_dilated | solution.py:23
  74.0 11.9 %fusion.122 = f32[1,368,512]{2,0,1:T(1,128)S(1)} fusion(bf16[1,504,512]{2,1,0:T(8,128)(2,1)S(1)} %copy-done.206, bf16[128,1,512]{2,0,1:T(8,128)(2,1)S(1)} %bitcast.619), kind=kOutput, calls=%fused_computation.238 | convolution fusion | flops 48234496 | bytes 1400832 | tf_op jit(solution)/shard_map/conv_general_dilated | solution.py:23
  86.0 11.7 %fusion.124 = f32[1,368,512]{2,0,1:T(1,128)S(1)} fusion(bf16[1,504,512]{2,1,0:T(8,128)(2,1)S(1)} %copy-done.207, bf16[128,1,512]{2,0,1:T(8,128)(2,1)S(1)} %bitcast.617), kind=kOutput, calls=%fused_computation.240 | convolution fusion | flops 48234496 | bytes 1400832 | tf_op jit(solution)/shard_map/conv_general_dilated | solution.py:23
  97.8 11.8 %fusion.120 = f32[1,368,512]{2,0,1:T(1,128)S(1)} fusion(bf16[1,504,512]{2,1,0:T(8,128)(2,1)S(1)} %fusion.115, bf16[128,1,512]{2,0,1:T(8,128)(2,1)S(1)} %bitcast.615), kind=kOutput, calls=%fused_computation.236 | convolution fusion | flops 48234496 | bytes 1400832 | tf_op jit(solution)/shard_map/conv_general_dilated | solution.py:23
  125.7 5.6 fusion.303
  144.2 13.4 %collective-permute-done.8 = bf16[512,1024]{1,0:T(8,128)(2,1)S(1)} collective-permute-done((bf16[512,1024]{1,0:T(8,128)(2,1)}, bf16[512,1024]{1,0:T(8,128)(2,1)S(1)}, u32[]{:S(2)}, u32[]{:S(2)}) %collective-permute-start.8) | collective-permute-done | bytes 1048608 | tf_op jit(solution)/shard_map/ppermute | solution.py:93
  159.7 22.4 %collective-permute-done.16 = bf16[512,1024]{1,0:T(8,128)(2,1)S(1)} collective-permute-done((bf16[512,1024]{1,0:T(8,128)(2,1)}, bf16[512,1024]{1,0:T(8,128)(2,1)S(1)}, u32[]{:S(2)}, u32[]{:S(2)}) %collective-permute-start.16) | collective-permute-done | bytes 1048608 | tf_op jit(solution)/shard_map/ppermute | solution.py:94
  189.2 13.4 %collective-permute-done.9 = bf16[512,1024]{1,0:T(8,128)(2,1)S(1)} collective-permute-done((bf16[512,1024]{1,0:T(8,128)(2,1)S(1)}, bf16[512,1024]{1,0:T(8,128)(2,1)S(1)}, u32[]{:S(2)}, u32[]{:S(2)}) %collective-permute-start.9) | collective-permute-done | bytes 1048608 | tf_op jit(solution)/shard_map/ppermute | solution.py:93
  204.8 22.2 %collective-permute-done.17 = bf16[512,1024]{1,0:T(8,128)(2,1)S(1)} collective-permute-done((bf16[512,1024]{1,0:T(8,128)(2,1)S(1)}, bf16[512,1024]{1,0:T(8,128)(2,1)S(1)}, u32[]{:S(2)}, u32[]{:S(2)}) %collective-permute-start.17) | collective-permute-done | bytes 1048608 | tf_op jit(solution)/shard_map/ppermute | solution.py:94
  232.8 3.5 collective-permute-done.10
  238.3 9.2 collective-permute-done.6
  255.4 16.6 %collective-permute-done.23 = bf16[512,1024]{1,0:T(8,128)(2,1)S(1)} collective-permute-done((bf16[512,1024]{1,0:T(8,128)(2,1)S(1)}, bf16[512,1024]{1,0:T(8,128)(2,1)S(1)}, u32[]{:S(2)}, u32[]{:S(2)}) %collective-permute-start.23) | collective-permute-done | bytes 1048608 | tf_op jit(solution)/shard_map/ppermute | solution.py:94
  274.0 20.4 %collective-permute-done.19 = bf16[512,1024]{1,0:T(8,128)(2,1)S(1)} collective-permute-done((bf16[512,1024]{1,0:T(8,128)(2,1)S(1)}, bf16[512,1024]{1,0:T(8,128)(2,1)S(1)}, u32[]{:S(2)}, u32[]{:S(2)}) %collective-permute-start.19) | collective-permute-done | bytes 1048608 | tf_op jit(solution)/shard_map/ppermute | solution.py:94
  299.7 17.2 %collective-permute-done.31 = bf16[512,1024]{1,0:T(8,128)(2,1)S(1)} collective-permute-done((bf16[512,1024]{1,0:T(8,128)(2,1)S(1)}, bf16[512,1024]{1,0:T(8,128)(2,1)S(1)}, u32[]{:S(2)}, u32[]{:S(2)}) %collective-permute-start.31) | collective-permute-done | bytes 1048608 | tf_op jit(solution)/shard_map/ppermute | solution.py:94
  319.0 20.4 %collective-permute-done.30 = bf16[512,1024]{1,0:T(8,128)(2,1)S(1)} collective-permute-done((bf16[512,1024]{1,0:T(8,128)(2,1)S(1)}, bf16[512,1024]{1,0:T(8,128)(2,1)S(1)}, u32[]{:S(2)}, u32[]{:S(2)}) %collective-permute-start.30) | collective-permute-done | bytes 1048608 | tf_op jit(solution)/shard_map/ppermute | solution.py:94
  346.5 15.4 %collective-permute-done.39 = bf16[512,1024]{1,0:T(8,128)(2,1)S(1)} collective-permute-done((bf16[512,1024]{1,0:T(8,128)(2,1)S(1)}, bf16[512,1024]{1,0:T(8,128)(2,1)S(1)}, u32[]{:S(2)}, u32[]{:S(2)}) %collective-permute-start.39) | collective-permute-done | bytes 1048608 | tf_op jit(solution)/shard_map/ppermute | solution.py:94
  364.1 20.3 %collective-permute-done.38 = bf16[512,1024]{1,0:T(8,128)(2,1)S(1)} collective-permute-done((bf16[512,1024]{1,0:T(8,128)(2,1)S(1)}, bf16[512,1024]{1,0:T(8,128)(2,1)S(1)}, u32[]{:S(2)}, u32[]{:S(2)}) %collective-permute-start.38) | collective-permute-done | bytes 1048608 | tf_op jit(solution)/shard_map/ppermute | solution.py:94
  390.2 5.3 collective-permute-done.47
  399.3 4.9 collective-permute-done.46
  411.5 4.5 fusion.170
  416.2 3.5 multiply_bitcast_fusion
  425.1 12.3 %fusion.106 = f32[1,384,512]{2,0,1:T(1,128)S(1)} fusion(bf16[1,511,512]{2,1,0:T(8,128)(2,1)S(1)} %slice_bitcast_fusion, bf16[128,1,512]{2,0,1:T(8,128)(2,1)S(1)} %copy-done.230), kind=kOutput, calls=%fused_computation.218 | convolution fusion | flops 50331648 | bytes 1440768 | tf_op jit(solution)/shard_map/conv_general_dilated | solution.py:23
  439.0 5.7 fusion.174
  444.8 3.4 multiply_bitcast_fusion.2
  448.3 12.3 %fusion.110 = f32[1,384,512]{2,0,1:T(1,128)S(1)} fusion(bf16[1,511,512]{2,1,0:T(8,128)(2,1)S(1)} %slice_bitcast_fusion.2, bf16[128,1,512]{2,0,1:T(8,128)(2,1)S(1)} %copy-done.228), kind=kOutput, calls=%fused_computation.222 | convolution fusion | flops 50331648 | bytes 1440768 | tf_op jit(solution)/shard_map/conv_general_dilated | solution.py:23
  461.7 4.5 fusion.176
  466.4 3.4 multiply_bitcast_fusion.3
  469.9 12.4 %fusion.112 = f32[1,384,512]{2,0,1:T(1,128)S(1)} fusion(bf16[1,511,512]{2,1,0:T(8,128)(2,1)S(1)} %slice_bitcast_fusion.3, bf16[128,1,512]{2,0,1:T(8,128)(2,1)S(1)} %copy-done.226), kind=kOutput, calls=%fused_computation.224 | convolution fusion | flops 50331648 | bytes 1440768 | tf_op jit(solution)/shard_map/conv_general_dilated | solution.py:23
  483.3 4.7 fusion.172
  488.2 3.4 multiply_bitcast_fusion.1
  491.6 12.4 %fusion.108 = f32[1,384,512]{2,0,1:T(1,128)S(1)} fusion(bf16[1,511,512]{2,1,0:T(8,128)(2,1)S(1)} %slice_bitcast_fusion.1, bf16[128,1,512]{2,0,1:T(8,128)(2,1)S(1)} %copy-done.224), kind=kOutput, calls=%fused_computation.220 | convolution fusion | flops 50331648 | bytes 1440768 | tf_op jit(solution)/shard_map/conv_general_dilated | solution.py:23
  505.0 13.6 %fusion.46 = bf16[1,128,512]{2,0,1:T(2,128)(2,1)S(1)} fusion(bf16[1,639,512]{2,1,0:T(8,128)(2,1)S(1)} %copy-done.197, bf16[512,1,512]{2,0,1:T(8,128)(2,1)S(1)} %bitcast.572), kind=kOutput, calls=%fused_computation.133 | convolution fusion | flops 67174400 | bytes 1309696 | tf_op jit(solution)/shard_map/conv_general_dilated | solution.py:23
  519.2 13.5 %fusion.49 = bf16[1,128,512]{2,0,1:T(2,128)(2,1)S(1)} fusion(bf16[1,639,512]{2,1,0:T(8,128)(2,1)S(1)} %copy-done.198, bf16[512,1,512]{2,0,1:T(8,128)(2,1)S(1)} %bitcast.571), kind=kOutput, calls=%fused_computation.134 | convolution fusion | flops 67174400 | bytes 1309696 | tf_op jit(solution)/shard_map/conv_general_dilated | solution.py:23
  534.4 13.6 %fusion.52 = bf16[1,128,512]{2,0,1:T(2,128)(2,1)S(1)} fusion(bf16[1,639,512]{2,1,0:T(8,128)(2,1)S(1)} %fusion.167, bf16[512,1,512]{2,0,1:T(8,128)(2,1)S(1)} %bitcast.573), kind=kOutput, calls=%fused_computation.135 | convolution fusion | flops 67174400 | bytes 1309696 | tf_op jit(solution)/shard_map/conv_general_dilated | solution.py:23
  549.0 13.6 %fusion.55 = bf16[1,128,512]{2,0,1:T(2,128)(2,1)S(1)} fusion(bf16[1,639,512]{2,1,0:T(8,128)(2,1)S(1)} %fusion.166, bf16[512,1,512]{2,0,1:T(8,128)(2,1)S(1)} %bitcast.570), kind=kOutput, calls=%fused_computation.136 | convolution fusion | flops 67174400 | bytes 1309696 | tf_op jit(solution)/shard_map/conv_general_dilated | solution.py:23
  565.7 4.1 fusion.181
  569.8 5.1 all-gather.15.cloned.1.call-done
  576.5 3.7 fusion.185
  580.9 34.9 %all-gather.13.cloned.1.call-done = bf16[1024,512]{1,0:T(8,128)(2,1)} async-done(((bf16[128,512]{1,0:T(8,128)(2,1)}), bf16[1024,512]{1,0:T(8,128)(2,1)}) %all-gather.13.cloned.1.call-update) | async-done | bytes 1048592 | tf_op jit(solution)/shard_map/all_gather | solution.py:140
  617.4 3.7 fusion.187
  621.8 34.9 %all-gather.17.cloned.1.call-done = bf16[1024,512]{1,0:T(8,128)(2,1)} async-done(((bf16[128,512]{1,0:T(8,128)(2,1)}), bf16[1024,512]{1,0:T(8,128)(2,1)}) %all-gather.17.cloned.1.call-update) | async-done | bytes 1048592 | tf_op jit(solution)/shard_map/all_gather | solution.py:140
  658.4 3.7 fusion.183
  682.9 30.6 %all_gather.46 = bf16[8,24,512]{2,1,0:T(8,128)(2,1)S(1)} all-gather(bf16[1,24,512]{2,1,0:T(8,128)(2,1)S(1)} %fusion.243), channel_id=1, replica_groups=mesh['ctx'=8,'tp'=4] {'ctx'}, dimensions={0}, use_global_device_ids=true | all-gather | bytes 221184 | tf_op jit(solution)/shard_map/all_gather | solution.py:150
  715.6 3.6 multiply_reduce_fusion.10
  720.1 30.6 %all_gather.49 = bf16[8,24,512]{2,1,0:T(8,128)(2,1)S(1)} all-gather(bf16[1,24,512]{2,1,0:T(8,128)(2,1)S(1)} %fusion.244), channel_id=1, replica_groups=mesh['ctx'=8,'tp'=4] {'ctx'}, dimensions={0}, use_global_device_ids=true | all-gather | bytes 221184 | tf_op jit(solution)/shard_map/all_gather | solution.py:150
  754.6 3.8 multiply_reduce_fusion.7
  759.8 30.6 %all_gather.52 = bf16[8,24,512]{2,1,0:T(8,128)(2,1)S(1)} all-gather(bf16[1,24,512]{2,1,0:T(8,128)(2,1)S(1)} %fusion.245), channel_id=1, replica_groups=mesh['ctx'=8,'tp'=4] {'ctx'}, dimensions={0}, use_global_device_ids=true | all-gather | bytes 221184 | tf_op jit(solution)/shard_map/all_gather | solution.py:150
  794.4 3.6 multiply_reduce_fusion.4
  798.8 30.6 %all_gather.55 = bf16[8,24,512]{2,1,0:T(8,128)(2,1)S(1)} all-gather(bf16[1,24,512]{2,1,0:T(8,128)(2,1)S(1)} %fusion.246), channel_id=1, replica_groups=mesh['ctx'=8,'tp'=4] {'ctx'}, dimensions={0}, use_global_device_ids=true | all-gather | bytes 221184 | tf_op jit(solution)/shard_map/all_gather | solution.py:150
  832.8 3.7 multiply_reduce_fusion.1
  836.6 3.3 fusion.298
  839.9 3.3 fusion.301
  843.2 3.3 fusion.295
  874.6 4.9 add_convert_fusion.6
  879.5 6.6 pad_maximum_fusion
  917.8 33.9 %all-reduce.3.cloned.1.call-done = (bf16[137,512]{1,0:T(8,128)(2,1)}, bf16[137,512]{1,0:T(8,128)(2,1)}, bf16[137,512]{1,0:T(8,128)(2,1)}, bf16[137,512]{1,0:T(8,128)(2,1)}) async-done(((bf16[137,512]{1,0:T(8,128)(2,1)}, bf16[137,512]{1,0:T(8,128)(2,1)}, bf16[137,512]{1,0:T(8,128)(2,1)}, bf16[137,512]{1,0:T(8,128)(2,1)}), (bf16[137,512]{1,0:T(8,128)(2,1)}, bf16[137,512]{1,0:T(8,128)(2,1)}, ...) | async-done | bytes 561168 | tf_op jit(solution)/shard_map/psum | solution.py:179
  971.2 4.9 collective-permute-done.25
  977.7 4.1 collective-permute-done.29
  983.3 4.1 collective-permute-done.33
  (865 shorter events, 256.4 us)
Async XLA Ops:
  7.2 400.8 %all-gather.11.cloned.1.call-start = ((), (), s32[]{:S(2)}) async-start(), calls=%async_computation | async-start | bytes 5603328 | tf_op jit(solution)/shard_map/all_gather | solution.py:79
  11.8 119.5 %collective-permute-start.3 = (bf16[512,1024]{1,0:T(8,128)(2,1)}, bf16[512,1024]{1,0:T(8,128)(2,1)}, u32[]{:S(2)}, u32[]{:S(2)}) collective-permute-start(bf16[512,1024]{1,0:T(8,128)(2,1)} %get-tuple-element.48), channel_id=1, source_target_pairs={{0,8},{8,16},{16,24},{24,28},{28,20},{20,12},{12,4},{4,0},{1,9},{9... | collective-permute-start | bytes 3145736 | tf_op jit(solution)/shard_map/ppermute | solution.py:93
  14.8 118.5 %collective-permute-start.15 = (bf16[512,1024]{1,0:T(8,128)(2,1)}, bf16[512,1024]{1,0:T(8,128)(2,1)}, u32[]{:S(2)}, u32[]{:S(2)}) collective-permute-start(bf16[512,1024]{1,0:T(8,128)(2,1)} %get-tuple-element.48), channel_id=1, source_target_pairs={{8,0},{16,8},{24,16},{28,24},{20,28},{12,20},{4,12},{0,4},{9,1},{1... | collective-permute-start | bytes 3145736 | tf_op jit(solution)/shard_map/ppermute | solution.py:94
  14.8 120.5 %collective-permute-start.2 = (bf16[512,1024]{1,0:T(8,128)(2,1)}, bf16[512,1024]{1,0:T(8,128)(2,1)}, u32[]{:S(2)}, u32[]{:S(2)}) collective-permute-start(bf16[512,1024]{1,0:T(8,128)(2,1)} %get-tuple-element.47), channel_id=1, source_target_pairs={{0,8},{8,16},{16,24},{24,28},{28,20},{20,12},{12,4},{4,0},{1,9},{9... | collective-permute-start | bytes 3145736 | tf_op jit(solution)/shard_map/ppermute | solution.py:93
  16.8 116.6 %collective-permute-start.14 = (bf16[512,1024]{1,0:T(8,128)(2,1)}, bf16[512,1024]{1,0:T(8,128)(2,1)}, u32[]{:S(2)}, u32[]{:S(2)}) collective-permute-start(bf16[512,1024]{1,0:T(8,128)(2,1)} %get-tuple-element.47), channel_id=1, source_target_pairs={{8,0},{16,8},{24,16},{28,24},{20,28},{12,20},{4,12},{0,4},{9,1},{1... | collective-permute-start | bytes 3145736 | tf_op jit(solution)/shard_map/ppermute | solution.py:94
  19.0 545.1 %all-gather.19.cloned.1.call-start = ((), (), s32[]{:S(2)}) async-start(), calls=%async_computation.4 | async-start | bytes 1179648 | tf_op jit(solution)/shard_map/all_gather | solution.py:140
  55.6 354.7 %copy-start.240 = (f32[3,1,512]{2,0,1:T(4,128)}, f32[3,1,512]{2,0,1:T(4,128)S(1)}, u32[]{:S(2)}) copy-start(f32[3,1,512]{2,0,1:T(4,128)S(1)} %copy.512) | copy-start | bytes 18436
  131.3 279.1 %copy-start.30 = (bf16[3,512,512]{2,1,0:T(8,128)(2,1)}, bf16[3,512,512]{2,1,0:T(8,128)(2,1)S(1)}, u32[]{:S(2)}) copy-start(bf16[3,512,512]{2,1,0:T(8,128)(2,1)S(1)} %get-tuple-element.30) | copy-start | bytes 4718596
  131.3 279.1 %copy-start.32 = (bf16[3,512,512]{2,1,0:T(8,128)(2,1)}, bf16[3,512,512]{2,1,0:T(8,128)(2,1)S(1)}, u32[]{:S(2)}) copy-start(bf16[3,512,512]{2,1,0:T(8,128)(2,1)S(1)} %get-tuple-element.32) | copy-start | bytes 4718596
  131.3 26.4 %collective-permute-start.8 = (bf16[512,1024]{1,0:T(8,128)(2,1)}, bf16[512,1024]{1,0:T(8,128)(2,1)S(1)}, u32[]{:S(2)}, u32[]{:S(2)}) collective-permute-start(bf16[512,1024]{1,0:T(8,128)(2,1)} %collective-permute-done.3), channel_id=1, source_target_pairs={{0,8},{8,16},{16,24},{24,28},{28,20},{20,12},{12,4},{4,0},{1,9},{9... | collective-permute-start | bytes 3145736 | tf_op jit(solution)/shard_map/ppermute | solution.py:93
  133.3 26.3 %collective-permute-start.20 = (bf16[512,1024]{1,0:T(8,128)(2,1)}, bf16[512,1024]{1,0:T(8,128)(2,1)S(1)}, u32[]{:S(2)}, u32[]{:S(2)}) collective-permute-start(bf16[512,1024]{1,0:T(8,128)(2,1)} %collective-permute-done.15), channel_id=1, source_target_pairs={{8,0},{16,8},{24,16},{28,24},{20,28},{12,20},{4,12},{0,4},{9,1},{1... | collective-permute-start | bytes 3145736 | tf_op jit(solution)/shard_map/ppermute | solution.py:94
  133.4 48.7 %collective-permute-start.16 = (bf16[512,1024]{1,0:T(8,128)(2,1)}, bf16[512,1024]{1,0:T(8,128)(2,1)S(1)}, u32[]{:S(2)}, u32[]{:S(2)}) collective-permute-start(bf16[512,1024]{1,0:T(8,128)(2,1)} %collective-permute-done.14), channel_id=1, source_target_pairs={{8,0},{16,8},{24,16},{28,24},{20,28},{12,20},{4,12},{0,4},{9,1},{1... | collective-permute-start | bytes 3145736 | tf_op jit(solution)/shard_map/ppermute | solution.py:94
  135.3 46.9 %collective-permute-start.4 = (bf16[512,1024]{1,0:T(8,128)(2,1)}, bf16[512,1024]{1,0:T(8,128)(2,1)S(1)}, u32[]{:S(2)}, u32[]{:S(2)}) collective-permute-start(bf16[512,1024]{1,0:T(8,128)(2,1)} %collective-permute-done.2), channel_id=1, source_target_pairs={{0,8},{8,16},{16,24},{24,28},{28,20},{20,12},{12,4},{4,0},{1,9},{9... | collective-permute-start | bytes 3145736 | tf_op jit(solution)/shard_map/ppermute | solution.py:93
  157.6 44.9 %collective-permute-start.9 = (bf16[512,1024]{1,0:T(8,128)(2,1)S(1)}, bf16[512,1024]{1,0:T(8,128)(2,1)S(1)}, u32[]{:S(2)}, u32[]{:S(2)}) collective-permute-start(bf16[512,1024]{1,0:T(8,128)(2,1)S(1)} %collective-permute-done.8), channel_id=1, source_target_pairs={{0,8},{8,16},{16,24},{24,28},{28,20},{20,12},{12,4},{4,0},{1,9},{9... | collective-permute-start | bytes 3145736 | tf_op jit(solution)/shard_map/ppermute | solution.py:93
  159.6 45.0 %collective-permute-start.21 = (bf16[512,1024]{1,0:T(8,128)(2,1)S(1)}, bf16[512,1024]{1,0:T(8,128)(2,1)S(1)}, u32[]{:S(2)}, u32[]{:S(2)}) collective-permute-start(bf16[512,1024]{1,0:T(8,128)(2,1)S(1)} %collective-permute-done.20), channel_id=1, source_target_pairs={{8,0},{16,8},{24,16},{28,24},{20,28},{12,20},{4,12},{0,4},{9,1},{1... | collective-permute-start | bytes 3145736 | tf_op jit(solution)/shard_map/ppermute | solution.py:94
  182.1 44.9 %collective-permute-start.17 = (bf16[512,1024]{1,0:T(8,128)(2,1)S(1)}, bf16[512,1024]{1,0:T(8,128)(2,1)S(1)}, u32[]{:S(2)}, u32[]{:S(2)}) collective-permute-start(bf16[512,1024]{1,0:T(8,128)(2,1)S(1)} %collective-permute-done.16), channel_id=1, source_target_pairs={{8,0},{16,8},{24,16},{28,24},{20,28},{12,20},{4,12},{0,4},{9,1},{1... | collective-permute-start | bytes 3145736 | tf_op jit(solution)/shard_map/ppermute | solution.py:94
  182.2 45.0 %collective-permute-start.5 = (bf16[512,1024]{1,0:T(8,128)(2,1)S(1)}, bf16[512,1024]{1,0:T(8,128)(2,1)S(1)}, u32[]{:S(2)}, u32[]{:S(2)}) collective-permute-start(bf16[512,1024]{1,0:T(8,128)(2,1)S(1)} %collective-permute-done.4), channel_id=1, source_target_pairs={{0,8},{8,16},{16,24},{24,28},{28,20},{20,12},{12,4},{4,0},{1,9},{9... | collective-permute-start | bytes 3145736 | tf_op jit(solution)/shard_map/ppermute | solution.py:93
  202.6 33.7 %collective-permute-start.10 = (bf16[512,512]{1,0:T(8,128)(2,1)S(1)}, bf16[512,512]{1,0:T(8,128)(2,1)S(1)}, u32[]{:S(2)}, u32[]{:S(2)}) collective-permute-start(bf16[512,512]{1,0:T(8,128)(2,1)S(1)} %slice.778), channel_id=1, source_target_pairs={{0,8},{8,16},{16,24},{24,28},{28,20},{20,12},{12,4},{4,0},{1,9},{9... | collective-permute-start | bytes 1572872 | tf_op jit(solution)/shard_map/ppermute | solution.py:96
  204.7 33.6 %collective-permute-start.22 = (bf16[512,512]{1,0:T(8,128)(2,1)S(1)}, bf16[512,512]{1,0:T(8,128)(2,1)S(1)}, u32[]{:S(2)}, u32[]{:S(2)}) collective-permute-start(bf16[512,512]{1,0:T(8,128)(2,1)S(1)} %slice.780), channel_id=1, source_target_pairs={{8,0},{16,8},{24,16},{28,24},{20,28},{12,20},{4,12},{0,4},{9,1},{1... | collective-permute-start | bytes 1572872 | tf_op jit(solution)/shard_map/ppermute | solution.py:97
  227.1 22.4 %collective-permute-start.18 = (bf16[512,512]{1,0:T(8,128)(2,1)S(1)}, bf16[512,512]{1,0:T(8,128)(2,1)S(1)}, u32[]{:S(2)}, u32[]{:S(2)}) collective-permute-start(bf16[512,512]{1,0:T(8,128)(2,1)S(1)} %slice.779), channel_id=1, source_target_pairs={{8,0},{16,8},{24,16},{28,24},{20,28},{12,20},{4,12},{0,4},{9,1},{1... | collective-permute-start | bytes 1572872 | tf_op jit(solution)/shard_map/ppermute | solution.py:97
  227.2 20.3 %collective-permute-start.6 = (bf16[512,512]{1,0:T(8,128)(2,1)S(1)}, bf16[512,512]{1,0:T(8,128)(2,1)S(1)}, u32[]{:S(2)}, u32[]{:S(2)}) collective-permute-start(bf16[512,512]{1,0:T(8,128)(2,1)S(1)} %slice.777), channel_id=1, source_target_pairs={{0,8},{8,16},{16,24},{24,28},{28,20},{20,12},{12,4},{4,0},{1,9},{9... | collective-permute-start | bytes 1572872 | tf_op jit(solution)/shard_map/ppermute | solution.py:96
  236.3 35.7 %collective-permute-start.11 = (bf16[512,1024]{1,0:T(8,128)(2,1)S(1)}, bf16[512,1024]{1,0:T(8,128)(2,1)S(1)}, u32[]{:S(2)}, u32[]{:S(2)}) collective-permute-start(bf16[512,1024]{1,0:T(8,128)(2,1)S(1)} %copy-done.184), channel_id=1, source_target_pairs={{0,8},{8,16},{16,24},{24,28},{28,20},{20,12},{12,4},{4,0},{1,9},{9... | collective-permute-start | bytes 3145736 | tf_op jit(solution)/shard_map/ppermute | solution.py:93
  238.3 33.7 %collective-permute-start.23 = (bf16[512,1024]{1,0:T(8,128)(2,1)S(1)}, bf16[512,1024]{1,0:T(8,128)(2,1)S(1)}, u32[]{:S(2)}, u32[]{:S(2)}) collective-permute-start(bf16[512,1024]{1,0:T(8,128)(2,1)S(1)} %copy-done.184), channel_id=1, source_target_pairs={{8,0},{16,8},{24,16},{28,24},{20,28},{12,20},{4,12},{0,4},{9,1},{1... | collective-permute-start | bytes 3145736 | tf_op jit(solution)/shard_map/ppermute | solution.py:94
  247.5 47.0 %collective-permute-start.7 = (bf16[512,1024]{1,0:T(8,128)(2,1)S(1)}, bf16[512,1024]{1,0:T(8,128)(2,1)S(1)}, u32[]{:S(2)}, u32[]{:S(2)}) collective-permute-start(bf16[512,1024]{1,0:T(8,128)(2,1)S(1)} %copy-done.183), channel_id=1, source_target_pairs={{0,8},{8,16},{16,24},{24,28},{28,20},{20,12},{12,4},{4,0},{1,9},{9... | collective-permute-start | bytes 3145736 | tf_op jit(solution)/shard_map/ppermute | solution.py:93
  249.5 44.9 %collective-permute-start.19 = (bf16[512,1024]{1,0:T(8,128)(2,1)S(1)}, bf16[512,1024]{1,0:T(8,128)(2,1)S(1)}, u32[]{:S(2)}, u32[]{:S(2)}) collective-permute-start(bf16[512,1024]{1,0:T(8,128)(2,1)S(1)} %copy-done.183), channel_id=1, source_target_pairs={{8,0},{16,8},{24,16},{28,24},{20,28},{12,20},{4,12},{0,4},{9,1},{1... | collective-permute-start | bytes 3145736 | tf_op jit(solution)/shard_map/ppermute | solution.py:94
  251.0 45.6 %copy-start.174 = (f32[512,512]{1,0:T(8,128)S(1)}, f32[512,512]{1,0:T(8,128)}, u32[]{:S(2)}) copy-start(f32[512,512]{1,0:T(8,128)} %fusion.158) | copy-start | bytes 3145732
  272.0 44.9 %collective-permute-start.31 = (bf16[512,1024]{1,0:T(8,128)(2,1)S(1)}, bf16[512,1024]{1,0:T(8,128)(2,1)S(1)}, u32[]{:S(2)}, u32[]{:S(2)}) collective-permute-start(bf16[512,1024]{1,0:T(8,128)(2,1)S(1)} %collective-permute-done.23), channel_id=1, source_target_pairs={{8,0},{16,8},{24,16},{28,24},{20,28},{12,20},{4,12},{0,4},{9,1},{1... | collective-permute-start | bytes 3145736 | tf_op jit(solution)/shard_map/ppermute | solution.py:94
  272.0 44.9 %collective-permute-start.27 = (bf16[512,1024]{1,0:T(8,128)(2,1)S(1)}, bf16[512,1024]{1,0:T(8,128)(2,1)S(1)}, u32[]{:S(2)}, u32[]{:S(2)}) collective-permute-start(bf16[512,1024]{1,0:T(8,128)(2,1)S(1)} %collective-permute-done.11), channel_id=1, source_target_pairs={{0,8},{8,16},{16,24},{24,28},{28,20},{20,12},{12,4},{4,0},{1,9},{9... | collective-permute-start | bytes 3145736 | tf_op jit(solution)/shard_map/ppermute | solution.py:93
  294.5 44.9 %collective-permute-start.30 = (bf16[512,1024]{1,0:T(8,128)(2,1)S(1)}, bf16[512,1024]{1,0:T(8,128)(2,1)S(1)}, u32[]{:S(2)}, u32[]{:S(2)}) collective-permute-start(bf16[512,1024]{1,0:T(8,128)(2,1)S(1)} %collective-permute-done.19), channel_id=1, source_target_pairs={{8,0},{16,8},{24,16},{28,24},{20,28},{12,20},{4,12},{0,4},{9,1},{1... | collective-permute-start | bytes 3145736 | tf_op jit(solution)/shard_map/ppermute | solution.py:94
  294.5 44.9 %collective-permute-start.26 = (bf16[512,1024]{1,0:T(8,128)(2,1)S(1)}, bf16[512,1024]{1,0:T(8,128)(2,1)S(1)}, u32[]{:S(2)}, u32[]{:S(2)}) collective-permute-start(bf16[512,1024]{1,0:T(8,128)(2,1)S(1)} %collective-permute-done.7), channel_id=1, source_target_pairs={{0,8},{8,16},{16,24},{24,28},{28,20},{20,12},{12,4},{4,0},{1,9},{9... | collective-permute-start | bytes 3145736 | tf_op jit(solution)/shard_map/ppermute | solution.py:93
  316.9 44.9 %collective-permute-start.39 = (bf16[512,1024]{1,0:T(8,128)(2,1)S(1)}, bf16[512,1024]{1,0:T(8,128)(2,1)S(1)}, u32[]{:S(2)}, u32[]{:S(2)}) collective-permute-start(bf16[512,1024]{1,0:T(8,128)(2,1)S(1)} %collective-permute-done.31), channel_id=1, source_target_pairs={{8,0},{16,8},{24,16},{28,24},{20,28},{12,20},{4,12},{0,4},{9,1},{1... | collective-permute-start | bytes 3145736 | tf_op jit(solution)/shard_map/ppermute | solution.py:94
  317.0 45.0 %collective-permute-start.35 = (bf16[512,1024]{1,0:T(8,128)(2,1)S(1)}, bf16[512,1024]{1,0:T(8,128)(2,1)S(1)}, u32[]{:S(2)}, u32[]{:S(2)}) collective-permute-start(bf16[512,1024]{1,0:T(8,128)(2,1)S(1)} %collective-permute-done.27), channel_id=1, source_target_pairs={{0,8},{8,16},{16,24},{24,28},{28,20},{20,12},{12,4},{4,0},{1,9},{9... | collective-permute-start | bytes 3145736 | tf_op jit(solution)/shard_map/ppermute | solution.py:93
  339.4 44.9 %collective-permute-start.38 = (bf16[512,1024]{1,0:T(8,128)(2,1)S(1)}, bf16[512,1024]{1,0:T(8,128)(2,1)S(1)}, u32[]{:S(2)}, u32[]{:S(2)}) collective-permute-start(bf16[512,1024]{1,0:T(8,128)(2,1)S(1)} %collective-permute-done.30), channel_id=1, source_target_pairs={{8,0},{16,8},{24,16},{28,24},{20,28},{12,20},{4,12},{0,4},{9,1},{1... | collective-permute-start | bytes 3145736 | tf_op jit(solution)/shard_map/ppermute | solution.py:94
  339.4 45.0 %collective-permute-start.34 = (bf16[512,1024]{1,0:T(8,128)(2,1)S(1)}, bf16[512,1024]{1,0:T(8,128)(2,1)S(1)}, u32[]{:S(2)}, u32[]{:S(2)}) collective-permute-start(bf16[512,1024]{1,0:T(8,128)(2,1)S(1)} %collective-permute-done.26), channel_id=1, source_target_pairs={{0,8},{8,16},{16,24},{24,28},{28,20},{20,12},{12,4},{4,0},{1,9},{9... | collective-permute-start | bytes 3145736 | tf_op jit(solution)/shard_map/ppermute | solution.py:93
  361.9 33.7 %collective-permute-start.47 = (bf16[512,512]{1,0:T(8,128)(2,1)S(1)}, bf16[512,512]{1,0:T(8,128)(2,1)S(1)}, u32[]{:S(2)}, u32[]{:S(2)}) collective-permute-start(bf16[512,512]{1,0:T(8,128)(2,1)S(1)} %slice.784), channel_id=1, source_target_pairs={{8,0},{16,8},{24,16},{28,24},{20,28},{12,20},{4,12},{0,4},{9,1},{1... | collective-permute-start | bytes 1572872 | tf_op jit(solution)/shard_map/ppermute | solution.py:97
  362.1 35.0 %collective-permute-start.43 = (bf16[512,512]{1,0:T(8,128)(2,1)S(1)}, bf16[512,512]{1,0:T(8,128)(2,1)S(1)}, u32[]{:S(2)}, u32[]{:S(2)}) collective-permute-start(bf16[512,512]{1,0:T(8,128)(2,1)S(1)} %slice.782), channel_id=1, source_target_pairs={{0,8},{8,16},{16,24},{24,28},{28,20},{20,12},{12,4},{4,0},{1,9},{9... | collective-permute-start | bytes 1572872 | tf_op jit(solution)/shard_map/ppermute | solution.py:96
  384.4 19.8 %collective-permute-start.46 = (bf16[512,512]{1,0:T(8,128)(2,1)S(1)}, bf16[512,512]{1,0:T(8,128)(2,1)S(1)}, u32[]{:S(2)}, u32[]{:S(2)}) collective-permute-start(bf16[512,512]{1,0:T(8,128)(2,1)S(1)} %slice.783), channel_id=1, source_target_pairs={{8,0},{16,8},{24,16},{28,24},{20,28},{12,20},{4,12},{0,4},{9,1},{1... | collective-permute-start | bytes 1572872 | tf_op jit(solution)/shard_map/ppermute | solution.py:97
  384.5 21.2 %collective-permute-start.42 = (bf16[512,512]{1,0:T(8,128)(2,1)S(1)}, bf16[512,512]{1,0:T(8,128)(2,1)S(1)}, u32[]{:S(2)}, u32[]{:S(2)}) collective-permute-start(bf16[512,512]{1,0:T(8,128)(2,1)S(1)} %slice.781), channel_id=1, source_target_pairs={{0,8},{8,16},{16,24},{24,28},{28,20},{20,12},{12,4},{4,0},{1,9},{9... | collective-permute-start | bytes 1572872 | tf_op jit(solution)/shard_map/ppermute | solution.py:96
  411.3 76.8 %copy-start.189 = (f32[3,8,512]{2,1,0:T(8,128)}, f32[3,8,512]{2,1,0:T(8,128)S(1)}, u32[]{:S(2)}) copy-start(f32[3,8,512]{2,1,0:T(8,128)S(1)} %get-tuple-element.29) | copy-start | bytes 147460
  438.4 136.5 %all-gather.15.cloned.1.call-start = ((), (), s32[]{:S(2)}) async-start(), calls=%async_computation.2 | async-start | bytes 1179648 | tf_op jit(solution)/shard_map/all_gather | solution.py:140
  448.2 85.3 %copy-start.70 = (bf16[512,512]{1,0:T(8,128)(2,1)}, bf16[512,512]{1,0:T(8,128)(2,1)S(1)}, u32[]{:S(2)}) copy-start(bf16[512,512]{1,0:T(8,128)(2,1)S(1)} %get-tuple-element.62) | copy-start | bytes 1572868
  469.8 78.4 %copy-start.72 = (bf16[512,512]{1,0:T(8,128)(2,1)}, bf16[512,512]{1,0:T(8,128)(2,1)S(1)}, u32[]{:S(2)}) copy-start(bf16[512,512]{1,0:T(8,128)(2,1)S(1)} %get-tuple-element.60) | copy-start | bytes 1572868
  491.6 71.7 %copy-start.74 = (bf16[512,512]{1,0:T(8,128)(2,1)}, bf16[512,512]{1,0:T(8,128)(2,1)S(1)}, u32[]{:S(2)}) copy-start(bf16[512,512]{1,0:T(8,128)(2,1)S(1)} %get-tuple-element.64) | copy-start | bytes 1572868
  534.3 81.6 %all-gather.13.cloned.1.call-start = ((), (), s32[]{:S(2)}) async-start(), calls=%async_computation.1 | async-start | bytes 1179648 | tf_op jit(solution)/shard_map/all_gather | solution.py:140
  548.9 107.9 %all-gather.17.cloned.1.call-start = ((), (), s32[]{:S(2)}) async-start(), calls=%async_computation.3 | async-start | bytes 1179648 | tf_op jit(solution)/shard_map/all_gather | solution.py:140
  564.0 387.7 %all-reduce.3.cloned.1.call-start = ((), (), s32[]{:S(2)}) async-start(), calls=%async_computation.5 | async-start | bytes 1179648 | tf_op jit(solution)/shard_map/psum | solution.py:179
  849.1 47.0 %collective-permute-start.48 = (bf16[2,128,512]{2,1,0:T(8,128)(2,1)}, bf16[2,128,512]{2,1,0:T(8,128)(2,1)}, u32[]{:S(2)}, u32[]{:S(2)}) collective-permute-start(bf16[2,128,512]{2,1,0:T(8,128)(2,1)} %dynamic-slice_bitcast_fusion.7), channel_id=1, source_target_pairs={{0,1},{1,0},{2,3},{3,2},{4,5},{5,4},{6,7},{7,6},{8,9},{9,8},{10,11... | collective-permute-start | bytes 786440 | tf_op jit(solution)/shard_map/ppermute | solution.py:193
  852.4 45.6 %collective-permute-start.44 = (bf16[2,128,512]{2,1,0:T(8,128)(2,1)}, bf16[2,128,512]{2,1,0:T(8,128)(2,1)}, u32[]{:S(2)}, u32[]{:S(2)}) collective-permute-start(bf16[2,128,512]{2,1,0:T(8,128)(2,1)} %dynamic-slice_bitcast_fusion.8), channel_id=1, source_target_pairs={{0,1},{1,0},{2,3},{3,2},{4,5},{5,4},{6,7},{7,6},{8,9},{9,8},{10,11... | collective-permute-start | bytes 786440 | tf_op jit(solution)/shard_map/ppermute | solution.py:193
  856.8 44.0 %collective-permute-start.40 = (bf16[2,128,1024]{2,1,0:T(8,128)(2,1)}, bf16[2,128,1024]{2,1,0:T(8,128)(2,1)}, u32[]{:S(2)}, u32[]{:S(2)}) collective-permute-start(bf16[2,128,1024]{2,1,0:T(8,128)(2,1)} %dynamic-slice_bitcast_fusion), channel_id=1, source_target_pairs={{0,1},{1,0},{2,3},{3,2},{4,5},{5,4},{6,7},{7,6},{8,9},{9,8},{10,11... | collective-permute-start | bytes 1572872 | tf_op jit(solution)/shard_map/ppermute | solution.py:193
  860.9 41.5 %collective-permute-start.36 = (bf16[2,128,1024]{2,1,0:T(8,128)(2,1)}, bf16[2,128,1024]{2,1,0:T(8,128)(2,1)}, u32[]{:S(2)}, u32[]{:S(2)}) collective-permute-start(bf16[2,128,1024]{2,1,0:T(8,128)(2,1)} %dynamic-slice_bitcast_fusion.1), channel_id=1, source_target_pairs={{0,1},{1,0},{2,3},{3,2},{4,5},{5,4},{6,7},{7,6},{8,9},{9,8},{10,11... | collective-permute-start | bytes 1572872 | tf_op jit(solution)/shard_map/ppermute | solution.py:193
  865.0 38.9 %collective-permute-start.32 = (bf16[2,128,1024]{2,1,0:T(8,128)(2,1)}, bf16[2,128,1024]{2,1,0:T(8,128)(2,1)}, u32[]{:S(2)}, u32[]{:S(2)}) collective-permute-start(bf16[2,128,1024]{2,1,0:T(8,128)(2,1)} %dynamic-slice_bitcast_fusion.2), channel_id=1, source_target_pairs={{0,1},{1,0},{2,3},{3,2},{4,5},{5,4},{6,7},{7,6},{8,9},{9,8},{10,11... | collective-permute-start | bytes 1572872 | tf_op jit(solution)/shard_map/ppermute | solution.py:193
  896.1 11.4 %collective-permute-start.28 = (bf16[2,128,1024]{2,1,0:T(8,128)(2,1)S(1)}, bf16[2,128,1024]{2,1,0:T(8,128)(2,1)S(1)}, u32[]{:S(2)}, u32[]{:S(2)}) collective-permute-start(bf16[2,128,1024]{2,1,0:T(8,128)(2,1)S(1)} %dynamic-slice_bitcast_fusion.3), channel_id=1, source_target_pairs={{0,1},{1,0},{2,3},{3,2},{4,5},{5,4},{6,7},{7,6},{8,9},{9,8},{10,11... | collective-permute-start | bytes 1572872 | tf_op jit(solution)/shard_map/ppermute | solution.py:193
  898.1 16.5 %collective-permute-start.24 = (bf16[2,128,1024]{2,1,0:T(8,128)(2,1)S(1)}, bf16[2,128,1024]{2,1,0:T(8,128)(2,1)S(1)}, u32[]{:S(2)}, u32[]{:S(2)}) collective-permute-start(bf16[2,128,1024]{2,1,0:T(8,128)(2,1)S(1)} %copy-done.203), channel_id=1, source_target_pairs={{0,1},{1,0},{2,3},{3,2},{4,5},{5,4},{6,7},{7,6},{8,9},{9,8},{10,11... | collective-permute-start | bytes 1572872 | tf_op jit(solution)/shard_map/ppermute | solution.py:193
  900.8 9.0 collective-permute-start.12
  902.3 9.9 collective-permute-start
  903.9 88.9 %collective-permute-start.49 = (bf16[1,128,512]{2,1,0:T(8,128)(2,1)}, bf16[1,128,512]{2,1,0:T(8,128)(2,1)}, u32[]{:S(2)}, u32[]{:S(2)}) collective-permute-start(bf16[1,128,512]{2,1,0:T(8,128)(2,1)} %constant_dynamic-slice_fusion), channel_id=1, source_target_pairs={{0,2},{1,3},{2,0},{3,1},{4,6},{5,7},{6,4},{7,5},{8,10},{9,11},{10,... | collective-permute-start | bytes 393224 | tf_op jit(solution)/shard_map/ppermute | solution.py:193
  907.5 84.3 %collective-permute-start.45 = (bf16[1,128,512]{2,1,0:T(8,128)(2,1)}, bf16[1,128,512]{2,1,0:T(8,128)(2,1)}, u32[]{:S(2)}, u32[]{:S(2)}) collective-permute-start(bf16[1,128,512]{2,1,0:T(8,128)(2,1)} %constant_dynamic-slice_fusion.1), channel_id=1, source_target_pairs={{0,2},{1,3},{2,0},{3,1},{4,6},{5,7},{6,4},{7,5},{8,10},{9,11},{10,... | collective-permute-start | bytes 393224 | tf_op jit(solution)/shard_map/ppermute | solution.py:193
  909.8 81.0 %collective-permute-start.41 = (bf16[1,128,1024]{2,1,0:T(8,128)(2,1)}, bf16[1,128,1024]{2,1,0:T(8,128)(2,1)}, u32[]{:S(2)}, u32[]{:S(2)}) collective-permute-start(bf16[1,128,1024]{2,1,0:T(8,128)(2,1)} %constant_dynamic-slice_fusion.2), channel_id=1, source_target_pairs={{0,2},{1,3},{2,0},{3,1},{4,6},{5,7},{6,4},{7,5},{8,10},{9,11},{10,... | collective-permute-start | bytes 786440 | tf_op jit(solution)/shard_map/ppermute | solution.py:193
  912.3 57.3 %collective-permute-start.13 = (bf16[1,128,1024]{2,1,0:T(8,128)(2,1)}, bf16[1,128,1024]{2,1,0:T(8,128)(2,1)}, u32[]{:S(2)}, u32[]{:S(2)}) collective-permute-start(bf16[1,128,1024]{2,1,0:T(8,128)(2,1)} %constant_dynamic-slice_fusion.7), channel_id=1, source_target_pairs={{0,2},{1,3},{2,0},{3,1},{4,6},{5,7},{6,4},{7,5},{8,10},{9,11},{10,... | collective-permute-start | bytes 786440 | tf_op jit(solution)/shard_map/ppermute | solution.py:193
  914.6 52.1 %collective-permute-start.1 = (bf16[1,128,1024]{2,1,0:T(8,128)(2,1)}, bf16[1,128,1024]{2,1,0:T(8,128)(2,1)}, u32[]{:S(2)}, u32[]{:S(2)}) collective-permute-start(bf16[1,128,1024]{2,1,0:T(8,128)(2,1)} %constant_dynamic-slice_fusion.8), channel_id=1, source_target_pairs={{0,2},{1,3},{2,0},{3,1},{4,6},{5,7},{6,4},{7,5},{8,10},{9,11},{10,... | collective-permute-start | bytes 786440 | tf_op jit(solution)/shard_map/ppermute | solution.py:193
  966.7 9.5 collective-permute-start.25
  969.6 12.2 %collective-permute-start.29 = (bf16[1,128,1024]{2,1,0:T(8,128)(2,1)}, bf16[1,128,1024]{2,1,0:T(8,128)(2,1)S(1)}, u32[]{:S(2)}, u32[]{:S(2)}) collective-permute-start(bf16[1,128,1024]{2,1,0:T(8,128)(2,1)} %constant_dynamic-slice_fusion.5), channel_id=1, source_target_pairs={{0,2},{1,3},{2,0},{3,1},{4,6},{5,7},{6,4},{7,5},{8,10},{9,11},{10,... | collective-permute-start | bytes 786440 | tf_op jit(solution)/shard_map/ppermute | solution.py:193
  976.2 11.2 %collective-permute-start.33 = (bf16[1,128,1024]{2,1,0:T(8,128)(2,1)}, bf16[1,128,1024]{2,1,0:T(8,128)(2,1)S(1)}, u32[]{:S(2)}, u32[]{:S(2)}) collective-permute-start(bf16[1,128,1024]{2,1,0:T(8,128)(2,1)} %constant_dynamic-slice_fusion.4), channel_id=1, source_target_pairs={{0,2},{1,3},{2,0},{3,1},{4,6},{5,7},{6,4},{7,5},{8,10},{9,11},{10,... | collective-permute-start | bytes 786440 | tf_op jit(solution)/shard_map/ppermute | solution.py:193
  981.8 8.9 collective-permute-start.37
  (247 other events, 1752.2 us)
Sparse Core Ops, SparseCore 0:
  19.1 104.8 all-gather.10
  438.5 40.4 all-gather.18
  534.4 40.5 all-gather.14
  576.9 38.8 all-gather.12
  617.8 38.8 all-gather.16
  879.6 72.0 all-reduce.2

commit v2 on v1

--- a/solution.py
+++ b/solution.py
@@ -81,8 +81,9 @@
     left_mixin = left_tail[:filt_len]
     left_raw = left_tail[filt_len:].reshape(3, edge_depth, channels)
 
-    arrived = []
-    for k in range(chunk_count):
+    arrived, rest_convs, lag_terms = [], [], []
+
+    def gather_chunk(k):
         own = out_weight[k * part : (k + 1) * part]
         up, down = own, own
         if k >= 2:
@@ -90,6 +91,10 @@
             down, _ = lax.optimization_barrier((own, arrived[k - 2][-1][2]))
         blocks = [(0, 0, own)]
         for step in range(1, half_ring):
+            if k >= 2 and step == 2:
+                up, rest_convs[k - 2] = lax.optimization_barrier((up, rest_convs[k - 2]))
+            if k >= 2 and step == half_ring - 1:
+                down, lag_terms[k - 2] = lax.optimization_barrier((down, lag_terms[k - 2]))
             up = lax.ppermute(up, "ctx", ahead)
             down = lax.ppermute(down, "ctx", behind)
             blocks += [(-step, 0, up), (step, 0, down)]
@@ -98,13 +103,17 @@
         blocks += [(-half_ring, 0, up), (-half_ring, width // 2, down)]
         arrived.append(blocks)
 
+    gather_chunk(0)
     grad_pieces = [
         lax.dynamic_slice_in_dim(out_grad, owner_of(offset) * width + first, block.shape[1], 1)
         for offset, first, block in arrived[0]
     ]
     mixed_sums = [None] * len(grad_pieces)
     grad_streams_parts, long_parts, short_parts = [], [], []
+    kept_values = []
     for k in range(chunk_count):
+        if k + 1 < chunk_count:
+            gather_chunk(k + 1)
         cut = slice(k * part, (k + 1) * part)
         raw = projected[:, :, cut]
         short_taps = short_filter[:, :, cut]
@@ -137,20 +146,54 @@
 
         grad_conv = (back_grad * act[0]).astype(jnp.bfloat16)
         grad_gate = back_grad * conv
-        got_head = lax.all_gather(grad_conv[:filt_len], "ctx", axis=0)
-        right_head = select_slot(got_head, reader, has_right)
-        mid_rows = rows_here - filt_len
-        gm_rest = depthwise(grad_conv[: rows_here - 1], filt)
+        rest_convs.append(depthwise(grad_conv[: rows_here - 1], filt))
+        lag_terms.append(depthwise(mixin_ext[1:], grad_conv))
+        kept_values.append((act, grad_conv, grad_gate, streams_ext))
+
+    heads = jnp.concatenate([values[1][:filt_len] for values in kept_values], 1)
+    right_heads = select_slot(lax.all_gather(heads, "ctx", axis=0), reader, has_right)
+    mid_rows = rows_here - filt_len
+    grad_acts = []
+    for k in range(chunk_count):
+        cut = slice(k * part, (k + 1) * part)
+        act, grad_conv, grad_gate, streams_ext = kept_values[k]
+        filt = long_filter[:, cut]
+        skip_row = skip_gain[None, cut]
+        gm_rest, right_head = rest_convs[k], right_heads[:, cut]
         gm_tail = depthwise(
             jnp.concatenate([grad_conv[mid_rows:], right_head], 0)[: 2 * filt_len - 1], filt
         )
         grad_mixin = jnp.concatenate([gm_rest, gm_tail], 0)
         grad_mixin = grad_mixin + skip_row * grad_conv.astype(jnp.float32)
         grad_act = jnp.stack([grad_gate, grad_mixin * act[2], grad_mixin * act[1]])
-        got_rows = lax.all_gather(
-            grad_act[:, :edge_depth].astype(jnp.bfloat16).reshape(3 * edge_depth, part), "ctx", axis=0
-        )
-        right_rows = select_slot(got_rows, reader, has_right).reshape(3, edge_depth, part)
+        grad_acts.append(grad_act)
+
+    share = rows_here // tp_count
+    mixed = jnp.zeros((share, width * ctx_count), jnp.bfloat16)
+    for j, (offset, first, block) in enumerate(arrived[0]):
+        piece = mixed_sums[j].astype(jnp.bfloat16).reshape(tp_count, share, block.shape[1])
+        bit = 1
+        while bit < tp_count:
+            pairs = piece.reshape(piece.shape[0] // 2, 2, share, block.shape[1])
+            mine = lax.rem(my_tp // bit, 2)
+            kept = lax.dynamic_index_in_dim(pairs, mine, 1, keepdims=False)
+            sent = lax.dynamic_index_in_dim(pairs, 1 - mine, 1, keepdims=False)
+            got = lax.ppermute(sent, "tp", [(i, i ^ bit) for i in range(tp_count)])
+            piece = (kept.astype(jnp.float32) + got.astype(jnp.float32)).astype(jnp.bfloat16)
+            bit *= 2
+        mixed = lax.dynamic_update_slice_in_dim(
+            mixed, piece[0], owner_of(offset) * width + first, 1
+        )
+    edge_grads = jnp.concatenate(
+        [g[:, :edge_depth].astype(jnp.bfloat16).reshape(3 * edge_depth, part) for g in grad_acts], 1
+    )
+    edge_grads, mixed = lax.optimization_barrier((edge_grads, mixed))
+    right_edges = select_slot(lax.all_gather(edge_grads, "ctx", axis=0), reader, has_right)
+    right_edges = right_edges.reshape(3, edge_depth, channels)
+    for k in range(chunk_count):
+        cut = slice(k * part, (k + 1) * part)
+        short_taps = short_filter[:, :, cut]
+        grad_act, streams_ext, right_rows = grad_acts[k], kept_values[k][3], right_edges[:, :, cut]
         grad_act_ext = jnp.concatenate([grad_act, right_rows.astype(jnp.float32)], 1)
         grad_streams = jnp.zeros(grad_act.shape, jnp.float32)
         for shift in range(taps):
@@ -172,7 +215,7 @@
             ],
             axis=1,
         )
-        long_terms = depthwise(mixin_ext[1:], grad_conv)
+        long_terms = lag_terms[k]
         both = jnp.concatenate(
             [long_terms.astype(jnp.bfloat16), short_terms.reshape(3 * taps, part).astype(jnp.bfloat16)], 0
         )
@@ -180,22 +223,6 @@
         long_parts.append(jnp.flip(total[:filt_len], 0))
         short_parts.append(total[filt_len:].reshape(3, taps, part))
 
-    share = rows_here // tp_count
-    mixed = jnp.zeros((share, width * ctx_count), jnp.bfloat16)
-    for j, (offset, first, block) in enumerate(arrived[0]):
-        piece = mixed_sums[j].astype(jnp.bfloat16).reshape(tp_count, share, block.shape[1])
-        bit = 1
-        while bit < tp_count:
-            pairs = piece.reshape(piece.shape[0] // 2, 2, share, block.shape[1])
-            mine = lax.rem(my_tp // bit, 2)
-            kept = lax.dynamic_index_in_dim(pairs, mine, 1, keepdims=False)
-            sent = lax.dynamic_index_in_dim(pairs, 1 - mine, 1, keepdims=False)
-            got = lax.ppermute(sent, "tp", [(i, i ^ bit) for i in range(tp_count)])
-            piece = (kept.astype(jnp.float32) + got.astype(jnp.float32)).astype(jnp.bfloat16)
-            bit *= 2
-        mixed = lax.dynamic_update_slice_in_dim(
-            mixed, piece[0], owner_of(offset) * width + first, 1
-        )
     return (
         mixed,
         jnp.concatenate(grad_streams_parts, 2),

time: 1010 us -> 823 us (0.81)
  blocking collectives: 122 us -> 32.3 us
  waiting for transfers between devices: 330 us -> 292 us
  local copies, waits for them, and re-layouts: 73.7 us -> 51.1 us
  other arithmetic: 103 us -> 82.2 us
  matrix products: 292 us -> 278 us
    all_gather x4 -> x1, blocking collectives: 122 us -> 32.3 us  [on_device(): lax.all_gather(edge_grads, 'ctx', axis=0)]
    all_gather x4 -> x1, waiting for transfers between devices: 75 us -> 16.4 us  [on_device(): lax.all_gather(heads, 'ctx', axis=0)]
    psum x1, waiting for transfers between devices: 33.9 us -> 65 us  [on_device(): total = lax.psum(both, 'ctx').astype(jnp.float32) * grad_scale]
    ppermute x32, waiting for transfers between devices: 205 us -> 174 us  [the longest x12 118 us: gather_chunk(): down = lax.ppermute(down, 'ctx', behind)]
    ppermute x18, waiting for transfers between devices: 16.4 us -> 37.2 us  [on_device(): got = lax.ppermute(sent, 'tp', [(i, i ^ bit) for i in range(tp_count)])]
    unnamed x539 -> x491, local copies, waits for them, and re-layouts: 32.2 us -> 27.1 us
  transfers between devices with their start and end apart: 56 -> 53, of which waited for: 22 -> 21; matrix products, arithmetic and copies ran while one was open for 36% -> 39% of each run, Pallas kernels for 0% -> 0%
where the time goes in v2:
time: 823 us; the launch traced here: 819 us
  waiting for transfers between devices  292 us (35%)
  matrix products  278 us (34%)
  other arithmetic  82.2 us (10%)
  local copies, waits for them, and re-layouts  51.1 us (6%)
  starting transfers between devices  50.9 us (6%)
  blocking collectives  32.3 us (4%)
  between operations  31.5 us (4%)
    conv_general_dilated x20, matrix products, depthwise(): lax.conv_general_dilated(signal[None], kernel[:, None, :], (1,), 'VALID',...  185 us
    ppermute x12, waiting for transfers between devices, gather_chunk(): down = lax.ppermute(down, 'ctx', behind)  118 us
    psum x1, waiting for transfers between devices, on_device(): total = lax.psum(both, 'ctx').astype(jnp.float32) * grad_scale  65 us
    dot_general x36, matrix products, on_device(): lax.dot_general(grad_pieces[j], block, (((1,), (1,)), ((), ())), preferre...  58.4 us
    ppermute x18, waiting for transfers between devices, on_device(): got = lax.ppermute(sent, 'tp', [(i, i ^ bit) for i in range(tp_count)])  37.2 us
    dot_general x36, matrix products, on_device(): out_term = jnp.dot(gated, block, preferred_element_type=jnp.float32)  34.7 us
    all_gather x1, blocking collectives, on_device(): lax.all_gather(edge_grads, 'ctx', axis=0)  32.3 us
    ppermute x12, waiting for transfers between devices, gather_chunk(): up = lax.ppermute(up, 'ctx', ahead)  30.8 us
  transfers between devices with their start and end apart: 53, of which 21 were waited for; matrix products, arithmetic and copies ran while one was open for 39% of the time, Pallas kernels for 0%

profile of v2, /device:TPU:0, one launch (start us, length us, event | category | flops | bytes accessed | tf_op | source)
XLA Modules:
  0.0 818.6 jit_solution(10622879169895741293)
XLA Ops:
  7.2 4.5 fusion.297
  11.8 3.0 collective-permute-start
  37.2 9.3 %multiply_add_fusion.2 = (f32[3,504,512]{2,1,0:T(8,128)S(1)}, f32[3,504,512]{2,1,0:T(8,128)S(1)}, f32[3,504,512]{2,1,0:T(8,128)}) fusion(bf16[3,512,2048]{2,1,0:T(8,128)(2,1)} %param.9, f32[3,512]{1,0:T(4,128)S(1)} %get-tuple-element.148, f32[3,512]{1,0:T(4,128)S(1)} %get-tuple-element.149, f32[3,512]{1,0:T(4,128)S(1)} %get-tuple-element.150, ...), kind=kLoop, calls=%fused_computation.51 | loop fusion | flops 18579456 | bytes 23279616 | tf_op jit(solution)/shard_map/add | solution.py:17
  46.8 11.7 %fusion.114 = f32[1,368,512]{2,0,1:T(1,128)S(1)} fusion(bf16[1,504,512]{2,1,0:T(8,128)(2,1)S(1)} %fusion.107, bf16[128,1,512]{2,0,1:T(8,128)(2,1)S(1)} %bitcast.604), kind=kOutput, calls=%fused_computation.236 | convolution fusion | flops 48234496 | bytes 1400832 | tf_op jit(solution)/shard_map/conv_general_dilated | solution.py:23
  61.0 12.1 %fusion.110 = f32[1,368,512]{2,0,1:T(1,128)S(1)} fusion(bf16[1,504,512]{2,1,0:T(8,128)(2,1)S(1)} %fusion.105, bf16[128,1,512]{2,0,1:T(8,128)(2,1)} %bitcast.600), kind=kOutput, calls=%fused_computation.232 | convolution fusion | flops 48234496 | bytes 1400832 | tf_op jit(solution)/shard_map/conv_general_dilated | solution.py:23
  75.9 11.7 %fusion.112 = f32[1,368,512]{2,0,1:T(1,128)S(1)} fusion(bf16[1,504,512]{2,1,0:T(8,128)(2,1)S(1)} %fusion.106, bf16[128,1,512]{2,0,1:T(8,128)(2,1)S(1)} %bitcast.606), kind=kOutput, calls=%fused_computation.234 | convolution fusion | flops 48234496 | bytes 1400832 | tf_op jit(solution)/shard_map/conv_general_dilated | solution.py:23
  89.3 4.0 multiply_add_fusion.1
  93.6 11.7 %fusion.108 = f32[1,368,512]{2,0,1:T(1,128)S(1)} fusion(bf16[1,504,512]{2,1,0:T(8,128)(2,1)S(1)} %fusion.104, bf16[128,1,512]{2,0,1:T(8,128)(2,1)S(1)} %bitcast.602), kind=kOutput, calls=%fused_computation.230 | convolution fusion | flops 48234496 | bytes 1400832 | tf_op jit(solution)/shard_map/conv_general_dilated | solution.py:23
  107.6 3.0 fusion.442
  113.6 3.0 fusion.156
  116.6 3.1 fusion.152
  120.3 2.1 fusion.154
  122.5 3.0 fusion.150
  125.4 2.2 fusion.296
  139.9 14.1 %collective-permute-done.3 = bf16[512,1024]{1,0:T(8,128)(2,1)S(1)} collective-permute-done((bf16[512,1024]{1,0:T(8,128)(2,1)}, bf16[512,1024]{1,0:T(8,128)(2,1)S(1)}, u32[]{:S(2)}, u32[]{:S(2)}) %collective-permute-start.3) | collective-permute-done | bytes 1048608 | tf_op jit(solution)/shard_map/ppermute | solution.py:99
  156.1 20.4 %collective-permute-done.12 = bf16[512,1024]{1,0:T(8,128)(2,1)S(1)} collective-permute-done((bf16[512,1024]{1,0:T(8,128)(2,1)}, bf16[512,1024]{1,0:T(8,128)(2,1)S(1)}, u32[]{:S(2)}, u32[]{:S(2)}) %collective-permute-start.12) | collective-permute-done | bytes 1048608 | tf_op jit(solution)/shard_map/ppermute | solution.py:99
  183.8 15.1 %collective-permute-done.5 = bf16[512,1024]{1,0:T(8,128)(2,1)S(1)} collective-permute-done((bf16[512,1024]{1,0:T(8,128)(2,1)S(1)}, bf16[512,1024]{1,0:T(8,128)(2,1)S(1)}, u32[]{:S(2)}, u32[]{:S(2)}) %collective-permute-start.5) | collective-permute-done | bytes 1048608 | tf_op jit(solution)/shard_map/ppermute | solution.py:99
  201.1 20.3 %collective-permute-done.14 = bf16[512,1024]{1,0:T(8,128)(2,1)S(1)} collective-permute-done((bf16[512,1024]{1,0:T(8,128)(2,1)S(1)}, bf16[512,1024]{1,0:T(8,128)(2,1)S(1)}, u32[]{:S(2)}, u32[]{:S(2)}) %collective-permute-start.14) | collective-permute-done | bytes 1048608 | tf_op jit(solution)/shard_map/ppermute | solution.py:99
  227.1 7.3 collective-permute-done.6
  236.5 9.2 %collective-permute-done.15 = bf16[512,512]{1,0:T(8,128)(2,1)S(1)} collective-permute-done((bf16[512,512]{1,0:T(8,128)(2,1)S(1)}, bf16[512,512]{1,0:T(8,128)(2,1)S(1)}, u32[]{:S(2)}, u32[]{:S(2)}) %collective-permute-start.15) | collective-permute-done | bytes 524320 | tf_op jit(solution)/shard_map/ppermute | solution.py:101
  253.6 12.9 %collective-permute-done.17 = bf16[512,1024]{1,0:T(8,128)(2,1)} collective-permute-done((bf16[512,1024]{1,0:T(8,128)(2,1)S(1)}, bf16[512,1024]{1,0:T(8,128)(2,1)}, u32[]{:S(2)}, u32[]{:S(2)}) %collective-permute-start.17) | collective-permute-done | bytes 1048608 | tf_op jit(solution)/shard_map/ppermute | solution.py:99
  268.2 20.7 %collective-permute-done.25 = bf16[512,1024]{1,0:T(8,128)(2,1)} collective-permute-done((bf16[512,1024]{1,0:T(8,128)(2,1)S(1)}, bf16[512,1024]{1,0:T(8,128)(2,1)}, u32[]{:S(2)}, u32[]{:S(2)}) %collective-permute-start.25) | collective-permute-done | bytes 1048608 | tf_op jit(solution)/shard_map/ppermute | solution.py:99
  300.3 4.5 fusion.167
  307.3 12.4 %fusion.102 = f32[1,384,512]{2,0,1:T(1,128)S(1)} fusion(bf16[1,511,512]{2,1,0:T(8,128)(2,1)S(1)} %slice_bitcast_fusion.4, bf16[128,1,512]{2,0,1:T(8,128)(2,1)S(1)} %copy-done.173), kind=kOutput, calls=%fused_computation.220 | convolution fusion | flops 50331648 | bytes 1440768 | tf_op jit(solution)/shard_map/conv_general_dilated | solution.py:23
  320.9 13.7 %fusion.42 = bf16[1,128,512]{2,0,1:T(2,128)(2,1)S(1)} fusion(bf16[1,639,512]{2,1,0:T(8,128)(2,1)S(1)} %fusion.160, bf16[512,1,512]{2,0,1:T(8,128)(2,1)S(1)} %bitcast.556), kind=kOutput, calls=%fused_computation.127 | convolution fusion | flops 67108864 | bytes 1309696 | tf_op jit(solution)/shard_map/conv_general_dilated | solution.py:23
  336.5 2.2 collective-permute-start.21
  338.7 4.5 fusion.165
  345.5 12.4 %fusion.100 = f32[1,384,512]{2,0,1:T(1,128)S(1)} fusion(bf16[1,511,512]{2,1,0:T(8,128)(2,1)S(1)} %slice_bitcast_fusion.3, bf16[128,1,512]{2,0,1:T(8,128)(2,1)S(1)} %copy-done.171), kind=kOutput, calls=%fused_computation.218 | convolution fusion | flops 50331648 | bytes 1440768 | tf_op jit(solution)/shard_map/conv_general_dilated | solution.py:23
  359.3 13.7 %fusion.40 = bf16[1,128,512]{2,0,1:T(2,128)(2,1)S(1)} fusion(bf16[1,639,512]{2,1,0:T(8,128)(2,1)S(1)} %slice_bitcast_fusion, bf16[512,1,512]{2,0,1:T(8,128)(2,1)S(1)} %bitcast.557), kind=kOutput, calls=%fused_computation.125 | convolution fusion | flops 67108864 | bytes 1309696 | tf_op jit(solution)/shard_map/conv_general_dilated | solution.py:23
  373.8 4.5 fusion.163
  380.2 4.5 fusion.161
  389.9 14.8 %collective-permute-done.29 = bf16[512,1024]{1,0:T(8,128)(2,1)S(1)} collective-permute-done((bf16[512,1024]{1,0:T(8,128)(2,1)}, bf16[512,1024]{1,0:T(8,128)(2,1)S(1)}, u32[]{:S(2)}, u32[]{:S(2)}) %collective-permute-start.29) | collective-permute-done | bytes 1048608 | tf_op jit(solution)/shard_map/ppermute | solution.py:99
  416.6 4.4 collective-permute-done.31
  421.5 11.4 %collective-permute-done.20 = bf16[512,1024]{1,0:T(8,128)(2,1)S(1)} collective-permute-done((bf16[512,1024]{1,0:T(8,128)(2,1)S(1)}, bf16[512,1024]{1,0:T(8,128)(2,1)S(1)}, u32[]{:S(2)}, u32[]{:S(2)}) %collective-permute-start.20) | collective-permute-done | bytes 1048608 | tf_op jit(solution)/shard_map/ppermute | solution.py:98
  433.2 19.4 %collective-permute-done.28 = bf16[512,1024]{1,0:T(8,128)(2,1)S(1)} collective-permute-done((bf16[512,1024]{1,0:T(8,128)(2,1)S(1)}, bf16[512,1024]{1,0:T(8,128)(2,1)S(1)}, u32[]{:S(2)}, u32[]{:S(2)}) %collective-permute-start.28) | collective-permute-done | bytes 1048608 | tf_op jit(solution)/shard_map/ppermute | solution.py:98
  454.9 3.3 collective-permute-done.22
  459.1 3.5 multiply_bitcast_fusion.1
  464.6 3.3 multiply_bitcast_fusion
  471.7 12.7 %fusion.98 = f32[1,384,512]{2,0,1:T(1,128)S(1)} fusion(bf16[1,511,512]{2,1,0:T(8,128)(2,1)S(1)} %slice_bitcast_fusion.2, bf16[128,1,512]{2,0,1:T(8,128)(2,1)} %get-tuple-element.94), kind=kOutput, calls=%fused_computation.216 | convolution fusion | flops 50331648 | bytes 1440768 | tf_op jit(solution)/shard_map/conv_general_dilated | solution.py:23
  485.4 12.3 %fusion.96 = f32[1,384,512]{2,0,1:T(1,128)S(1)} fusion(bf16[1,511,512]{2,1,0:T(8,128)(2,1)S(1)} %slice_bitcast_fusion.1, bf16[128,1,512]{2,0,1:T(8,128)(2,1)S(1)} %copy-done.168), kind=kOutput, calls=%fused_computation.214 | convolution fusion | flops 50331648 | bytes 1440768 | tf_op jit(solution)/shard_map/conv_general_dilated | solution.py:23
  498.8 13.6 %fusion.38 = bf16[1,128,512]{2,0,1:T(2,128)(2,1)S(1)} fusion(bf16[1,639,512]{2,1,0:T(8,128)(2,1)S(1)} %copy-done.146, bf16[512,1,512]{2,0,1:T(8,128)(2,1)S(1)} %bitcast.554), kind=kOutput, calls=%fused_computation.123 | convolution fusion | flops 67108864 | bytes 1309696 | tf_op jit(solution)/shard_map/conv_general_dilated | solution.py:23
  513.0 14.0 %fusion.36 = bf16[1,128,512]{2,0,1:T(2,128)(2,1)S(1)} fusion(bf16[1,639,512]{2,1,0:T(8,128)(2,1)S(1)} %copy-done.145, bf16[512,1,512]{2,0,1:T(8,128)(2,1)S(1)} %bitcast.555), kind=kOutput, calls=%fused_computation.121 | convolution fusion | flops 67108864 | bytes 1309696 | tf_op jit(solution)/shard_map/conv_general_dilated | solution.py:23
  527.6 16.4 %all-gather.8.cloned.1.call-done = bf16[1024,2048]{1,0:T(8,128)(2,1)} async-done(((bf16[128,2048]{1,0:T(8,128)(2,1)}), bf16[1024,2048]{1,0:T(8,128)(2,1)}) %all-gather.8.cloned.1.call-update) | async-done | bytes 4194320 | tf_op jit(solution)/shard_map/all_gather | solution.py:154
  546.6 4.2 fusion.178
  550.9 3.7 fusion.176
  554.7 3.7 fusion.174
  558.5 3.7 fusion.172
  575.2 3.3 multiply_reduce_fusion.11
  598.6 2.1 add_convert_fusion.2
  616.6 2.1 add_convert_fusion.4
  630.8 18.2 %collective-permute-done.33 = bf16[1,128,1024]{2,1,0:T(8,128)(2,1)S(1)} collective-permute-done((bf16[1,128,1024]{2,1,0:T(8,128)(2,1)S(1)}, bf16[1,128,1024]{2,1,0:T(8,128)(2,1)S(1)}, u32[]{:S(2)}, u32[]{:S(2)}) %collective-permute-start.33) | collective-permute-done | bytes 262176 | tf_op jit(solution)/shard_map/ppermute | solution.py:181
  651.5 6.8 collective-permute-done.37
  659.8 4.1 collective-permute-done.39
  665.4 4.1 collective-permute-done.41
  669.6 3.9 collective-permute-done.43
  673.8 32.3 %all-gather.2 = bf16[192,2048]{1,0:T(8,128)(2,1)S(1)} all-gather(bf16[24,2048]{1,0:T(8,128)(2,1)S(1)} %pad_maximum_fusion.35), channel_id=4, replica_groups=mesh['ctx'=8,'tp'=4] {'ctx'}, dimensions={0}, use_global_device_ids=true | all-gather | bytes 884736 | tf_op jit(solution)/shard_map/all_gather | solution.py:191
  708.2 3.2 multiply_reduce_fusion.10
  711.5 2.4 pad_maximum_fusion.2
  714.8 2.9 multiply_reduce_fusion.7
  718.4 2.1 pad_maximum_fusion.3
  721.1 3.0 multiply_reduce_fusion.4
  726.8 2.9 multiply_reduce_fusion.1
  734.8 6.5 pad_maximum_fusion
  741.4 65.0 %all-reduce.3.cloned.1.call-done = (bf16[137,512]{1,0:T(8,128)(2,1)}, bf16[137,512]{1,0:T(8,128)(2,1)}, bf16[137,512]{1,0:T(8,128)(2,1)}, bf16[137,512]{1,0:T(8,128)(2,1)}) async-done(((bf16[137,512]{1,0:T(8,128)(2,1)}, bf16[137,512]{1,0:T(8,128)(2,1)}, bf16[137,512]{1,0:T(8,128)(2,1)}, bf16[137,512]{1,0:T(8,128)(2,1)}), (bf16[137,512]{1,0:T(8,128)(2,1)}, bf16[137,512]{1,0:T(8,128)(2,1)}, ...) | async-done | bytes 561168 | tf_op jit(solution)/shard_map/psum | solution.py:222
  (807 shorter events, 201.0 us)
Async XLA Ops:
  7.2 289.1 %all-gather.6.cloned.1.call-start = ((), (), s32[]{:S(2)}) async-start(), calls=%async_computation | async-start | bytes 5603328 | tf_op jit(solution)/shard_map/all_gather | solution.py:79
  11.8 117.7 %collective-permute-start = (bf16[512,1024]{1,0:T(8,128)(2,1)}, bf16[512,1024]{1,0:T(8,128)(2,1)}, u32[]{:S(2)}, u32[]{:S(2)}) collective-permute-start(bf16[512,1024]{1,0:T(8,128)(2,1)} %get-tuple-element.67), channel_id=1, source_target_pairs={{0,8},{8,16},{16,24},{24,28},{28,20},{20,12},{12,4},{4,0},{1,9},{9... | collective-permute-start | bytes 3145736 | tf_op jit(solution)/shard_map/ppermute | solution.py:98
  14.8 112.8 %collective-permute-start.1 = (bf16[512,1024]{1,0:T(8,128)(2,1)}, bf16[512,1024]{1,0:T(8,128)(2,1)}, u32[]{:S(2)}, u32[]{:S(2)}) collective-permute-start(bf16[512,1024]{1,0:T(8,128)(2,1)} %get-tuple-element.67), channel_id=1, source_target_pairs={{8,0},{16,8},{24,16},{28,24},{20,28},{12,20},{4,12},{0,4},{9,1},{1... | collective-permute-start | bytes 3145736 | tf_op jit(solution)/shard_map/ppermute | solution.py:99
  14.8 116.7 %collective-permute-start.9 = (bf16[512,1024]{1,0:T(8,128)(2,1)}, bf16[512,1024]{1,0:T(8,128)(2,1)}, u32[]{:S(2)}, u32[]{:S(2)}) collective-permute-start(bf16[512,1024]{1,0:T(8,128)(2,1)} %get-tuple-element.70), channel_id=1, source_target_pairs={{0,8},{8,16},{16,24},{24,28},{28,20},{20,12},{12,4},{4,0},{1,9},{9... | collective-permute-start | bytes 3145736 | tf_op jit(solution)/shard_map/ppermute | solution.py:98
  16.8 112.9 %collective-permute-start.10 = (bf16[512,1024]{1,0:T(8,128)(2,1)}, bf16[512,1024]{1,0:T(8,128)(2,1)}, u32[]{:S(2)}, u32[]{:S(2)}) collective-permute-start(bf16[512,1024]{1,0:T(8,128)(2,1)} %get-tuple-element.70), channel_id=1, source_target_pairs={{8,0},{16,8},{24,16},{28,24},{20,28},{12,20},{4,12},{0,4},{9,1},{1... | collective-permute-start | bytes 3145736 | tf_op jit(solution)/shard_map/ppermute | solution.py:99
  19.1 524.9 %all-gather.8.cloned.1.call-start = ((), (), s32[]{:S(2)}) async-start(), calls=%async_computation.1 | async-start | bytes 4718592 | tf_op jit(solution)/shard_map/all_gather | solution.py:154
  34.6 264.2 %copy-start.205 = (f32[3,1,512]{2,0,1:T(4,128)}, f32[3,1,512]{2,0,1:T(4,128)S(1)}, u32[]{:S(2)}) copy-start(f32[3,1,512]{2,0,1:T(4,128)S(1)} %copy.293) | copy-start | bytes 18436
  34.6 264.2 %copy-start.190 = (f32[3,1,512]{2,0,1:T(4,128)}, f32[3,1,512]{2,0,1:T(4,128)S(1)}, u32[]{:S(2)}) copy-start(f32[3,1,512]{2,0,1:T(4,128)S(1)} %copy.294) | copy-start | bytes 18436
  37.1 261.7 %copy-start.201 = (f32[3,512]{1,0:T(4,128)}, f32[3,512]{1,0:T(4,128)S(1)}, u32[]{:S(2)}) copy-start(f32[3,512]{1,0:T(4,128)S(1)} %get-tuple-element.154) | copy-start | bytes 18436
  37.1 261.7 %copy-start.203 = (f32[3,512]{1,0:T(4,128)}, f32[3,512]{1,0:T(4,128)S(1)}, u32[]{:S(2)}) copy-start(f32[3,512]{1,0:T(4,128)S(1)} %get-tuple-element.155) | copy-start | bytes 18436
  89.3 209.5 %copy-start.207 = (f32[3,512]{1,0:T(4,128)}, f32[3,512]{1,0:T(4,128)S(1)}, u32[]{:S(2)}) copy-start(f32[3,512]{1,0:T(4,128)S(1)} %get-tuple-element.146) | copy-start | bytes 18436
  89.3 209.5 %copy-start.209 = (f32[3,512]{1,0:T(4,128)}, f32[3,512]{1,0:T(4,128)S(1)}, u32[]{:S(2)}) copy-start(f32[3,512]{1,0:T(4,128)S(1)} %get-tuple-element.147) | copy-start | bytes 18436
  107.6 197.3 %copy-start.218 = (f32[512]{0:T(512)}, f32[512]{0:T(512)S(1)}, u32[]{:S(2)}) copy-start(f32[512]{0:T(512)S(1)} %get-tuple-element.134) | copy-start | bytes 6148
  107.6 235.7 %copy-start.216 = (f32[512]{0:T(512)}, f32[512]{0:T(512)S(1)}, u32[]{:S(2)}) copy-start(f32[512]{0:T(512)S(1)} %get-tuple-element.135) | copy-start | bytes 6148
  127.6 171.2 %copy-start.30 = (bf16[3,512,512]{2,1,0:T(8,128)(2,1)}, bf16[3,512,512]{2,1,0:T(8,128)(2,1)S(1)}, u32[]{:S(2)}) copy-start(bf16[3,512,512]{2,1,0:T(8,128)(2,1)S(1)} %get-tuple-element.53) | copy-start | bytes 4718596
  127.6 207.7 %copy-start.32 = (bf16[3,512,512]{2,1,0:T(8,128)(2,1)}, bf16[3,512,512]{2,1,0:T(8,128)(2,1)S(1)}, u32[]{:S(2)}) copy-start(bf16[3,512,512]{2,1,0:T(8,128)(2,1)S(1)} %get-tuple-element.50) | copy-start | bytes 4718596
  127.6 26.4 %collective-permute-start.3 = (bf16[512,1024]{1,0:T(8,128)(2,1)}, bf16[512,1024]{1,0:T(8,128)(2,1)S(1)}, u32[]{:S(2)}, u32[]{:S(2)}) collective-permute-start(bf16[512,1024]{1,0:T(8,128)(2,1)} %collective-permute-done.1), channel_id=1, source_target_pairs={{8,0},{16,8},{24,16},{28,24},{20,28},{12,20},{4,12},{0,4},{9,1},{1... | collective-permute-start | bytes 3145736 | tf_op jit(solution)/shard_map/ppermute | solution.py:99
  129.5 26.3 %collective-permute-start.2 = (bf16[512,1024]{1,0:T(8,128)(2,1)}, bf16[512,1024]{1,0:T(8,128)(2,1)S(1)}, u32[]{:S(2)}, u32[]{:S(2)}) collective-permute-start(bf16[512,1024]{1,0:T(8,128)(2,1)} %collective-permute-done), channel_id=1, source_target_pairs={{0,8},{8,16},{16,24},{24,28},{28,20},{20,12},{12,4},{4,0},{1,9},{9... | collective-permute-start | bytes 3145736 | tf_op jit(solution)/shard_map/ppermute | solution.py:98
  129.7 46.7 %collective-permute-start.12 = (bf16[512,1024]{1,0:T(8,128)(2,1)}, bf16[512,1024]{1,0:T(8,128)(2,1)S(1)}, u32[]{:S(2)}, u32[]{:S(2)}) collective-permute-start(bf16[512,1024]{1,0:T(8,128)(2,1)} %collective-permute-done.10), channel_id=1, source_target_pairs={{8,0},{16,8},{24,16},{28,24},{20,28},{12,20},{4,12},{0,4},{9,1},{1... | collective-permute-start | bytes 3145736 | tf_op jit(solution)/shard_map/ppermute | solution.py:99
  131.5 46.7 %collective-permute-start.11 = (bf16[512,1024]{1,0:T(8,128)(2,1)}, bf16[512,1024]{1,0:T(8,128)(2,1)S(1)}, u32[]{:S(2)}, u32[]{:S(2)}) collective-permute-start(bf16[512,1024]{1,0:T(8,128)(2,1)} %collective-permute-done.9), channel_id=1, source_target_pairs={{0,8},{8,16},{16,24},{24,28},{28,20},{20,12},{12,4},{4,0},{1,9},{9... | collective-permute-start | bytes 3145736 | tf_op jit(solution)/shard_map/ppermute | solution.py:98
  154.0 44.9 %collective-permute-start.5 = (bf16[512,1024]{1,0:T(8,128)(2,1)S(1)}, bf16[512,1024]{1,0:T(8,128)(2,1)S(1)}, u32[]{:S(2)}, u32[]{:S(2)}) collective-permute-start(bf16[512,1024]{1,0:T(8,128)(2,1)S(1)} %collective-permute-done.3), channel_id=1, source_target_pairs={{8,0},{16,8},{24,16},{28,24},{20,28},{12,20},{4,12},{0,4},{9,1},{1... | collective-permute-start | bytes 3145736 | tf_op jit(solution)/shard_map/ppermute | solution.py:99
  155.8 45.0 %collective-permute-start.4 = (bf16[512,1024]{1,0:T(8,128)(2,1)S(1)}, bf16[512,1024]{1,0:T(8,128)(2,1)S(1)}, u32[]{:S(2)}, u32[]{:S(2)}) collective-permute-start(bf16[512,1024]{1,0:T(8,128)(2,1)S(1)} %collective-permute-done.2), channel_id=1, source_target_pairs={{0,8},{8,16},{16,24},{24,28},{28,20},{20,12},{12,4},{4,0},{1,9},{9... | collective-permute-start | bytes 3145736 | tf_op jit(solution)/shard_map/ppermute | solution.py:98
  176.5 44.9 %collective-permute-start.14 = (bf16[512,1024]{1,0:T(8,128)(2,1)S(1)}, bf16[512,1024]{1,0:T(8,128)(2,1)S(1)}, u32[]{:S(2)}, u32[]{:S(2)}) collective-permute-start(bf16[512,1024]{1,0:T(8,128)(2,1)S(1)} %collective-permute-done.12), channel_id=1, source_target_pairs={{8,0},{16,8},{24,16},{28,24},{20,28},{12,20},{4,12},{0,4},{9,1},{1... | collective-permute-start | bytes 3145736 | tf_op jit(solution)/shard_map/ppermute | solution.py:99
  178.3 45.0 %collective-permute-start.13 = (bf16[512,1024]{1,0:T(8,128)(2,1)S(1)}, bf16[512,1024]{1,0:T(8,128)(2,1)S(1)}, u32[]{:S(2)}, u32[]{:S(2)}) collective-permute-start(bf16[512,1024]{1,0:T(8,128)(2,1)S(1)} %collective-permute-done.11), channel_id=1, source_target_pairs={{0,8},{8,16},{16,24},{24,28},{28,20},{20,12},{12,4},{4,0},{1,9},{9... | collective-permute-start | bytes 3145736 | tf_op jit(solution)/shard_map/ppermute | solution.py:98
  199.0 35.7 %collective-permute-start.7 = (bf16[512,512]{1,0:T(8,128)(2,1)S(1)}, bf16[512,512]{1,0:T(8,128)(2,1)S(1)}, u32[]{:S(2)}, u32[]{:S(2)}) collective-permute-start(bf16[512,512]{1,0:T(8,128)(2,1)S(1)} %slice.787), channel_id=1, source_target_pairs={{8,0},{16,8},{24,16},{28,24},{20,28},{12,20},{4,12},{0,4},{9,1},{1... | collective-permute-start | bytes 1572872 | tf_op jit(solution)/shard_map/ppermute | solution.py:102
  200.9 33.6 %collective-permute-start.6 = (bf16[512,512]{1,0:T(8,128)(2,1)S(1)}, bf16[512,512]{1,0:T(8,128)(2,1)S(1)}, u32[]{:S(2)}, u32[]{:S(2)}) collective-permute-start(bf16[512,512]{1,0:T(8,128)(2,1)S(1)} %slice.786), channel_id=1, source_target_pairs={{0,8},{8,16},{16,24},{24,28},{28,20},{20,12},{12,4},{4,0},{1,9},{9... | collective-permute-start | bytes 1572872 | tf_op jit(solution)/shard_map/ppermute | solution.py:101
  221.4 24.5 %collective-permute-start.16 = (bf16[512,512]{1,0:T(8,128)(2,1)S(1)}, bf16[512,512]{1,0:T(8,128)(2,1)S(1)}, u32[]{:S(2)}, u32[]{:S(2)}) collective-permute-start(bf16[512,512]{1,0:T(8,128)(2,1)S(1)} %slice.803), channel_id=1, source_target_pairs={{8,0},{16,8},{24,16},{28,24},{20,28},{12,20},{4,12},{0,4},{9,1},{1... | collective-permute-start | bytes 1572872 | tf_op jit(solution)/shard_map/ppermute | solution.py:102
  223.4 22.3 %collective-permute-start.15 = (bf16[512,512]{1,0:T(8,128)(2,1)S(1)}, bf16[512,512]{1,0:T(8,128)(2,1)S(1)}, u32[]{:S(2)}, u32[]{:S(2)}) collective-permute-start(bf16[512,512]{1,0:T(8,128)(2,1)S(1)} %slice.802), channel_id=1, source_target_pairs={{0,8},{8,16},{16,24},{24,28},{28,20},{20,12},{12,4},{4,0},{1,9},{9... | collective-permute-start | bytes 1572872 | tf_op jit(solution)/shard_map/ppermute | solution.py:101
  234.4 56.5 %collective-permute-start.8 = (bf16[512,1024]{1,0:T(8,128)(2,1)S(1)}, bf16[512,1024]{1,0:T(8,128)(2,1)S(1)}, u32[]{:S(2)}, u32[]{:S(2)}) collective-permute-start(bf16[512,1024]{1,0:T(8,128)(2,1)S(1)} %copy-done.138), channel_id=1, source_target_pairs={{0,8},{8,16},{16,24},{24,28},{28,20},{20,12},{12,4},{4,0},{1,9},{9... | collective-permute-start | bytes 3145736 | tf_op jit(solution)/shard_map/ppermute | solution.py:98
  234.7 31.7 %collective-permute-start.17 = (bf16[512,1024]{1,0:T(8,128)(2,1)S(1)}, bf16[512,1024]{1,0:T(8,128)(2,1)}, u32[]{:S(2)}, u32[]{:S(2)}) collective-permute-start(bf16[512,1024]{1,0:T(8,128)(2,1)S(1)} %copy-done.138), channel_id=1, source_target_pairs={{8,0},{16,8},{24,16},{28,24},{20,28},{12,20},{4,12},{0,4},{9,1},{1... | collective-permute-start | bytes 3145736 | tf_op jit(solution)/shard_map/ppermute | solution.py:99
  245.7 47.9 %collective-permute-start.24 = (bf16[512,1024]{1,0:T(8,128)(2,1)S(1)}, bf16[512,1024]{1,0:T(8,128)(2,1)S(1)}, u32[]{:S(2)}, u32[]{:S(2)}) collective-permute-start(bf16[512,1024]{1,0:T(8,128)(2,1)S(1)} %copy-done.137), channel_id=1, source_target_pairs={{0,8},{8,16},{16,24},{24,28},{28,20},{20,12},{12,4},{4,0},{1,9},{9... | collective-permute-start | bytes 3145736 | tf_op jit(solution)/shard_map/ppermute | solution.py:98
  245.9 43.0 %collective-permute-start.25 = (bf16[512,1024]{1,0:T(8,128)(2,1)S(1)}, bf16[512,1024]{1,0:T(8,128)(2,1)}, u32[]{:S(2)}, u32[]{:S(2)}) collective-permute-start(bf16[512,1024]{1,0:T(8,128)(2,1)S(1)} %copy-done.137), channel_id=1, source_target_pairs={{8,0},{16,8},{24,16},{28,24},{20,28},{12,20},{4,12},{0,4},{9,1},{1... | collective-permute-start | bytes 3145736 | tf_op jit(solution)/shard_map/ppermute | solution.py:99
  266.4 69.9 %collective-permute-start.19 = (bf16[512,1024]{1,0:T(8,128)(2,1)}, bf16[512,1024]{1,0:T(8,128)(2,1)}, u32[]{:S(2)}, u32[]{:S(2)}) collective-permute-start(bf16[512,1024]{1,0:T(8,128)(2,1)} %collective-permute-done.17), channel_id=1, source_target_pairs={{8,0},{16,8},{24,16},{28,24},{20,28},{12,20},{4,12},{0,4},{9,1},{1... | collective-permute-start | bytes 3145736 | tf_op jit(solution)/shard_map/ppermute | solution.py:99
  288.9 89.4 %collective-permute-start.27 = (bf16[512,1024]{1,0:T(8,128)(2,1)}, bf16[512,1024]{1,0:T(8,128)(2,1)}, u32[]{:S(2)}, u32[]{:S(2)}) collective-permute-start(bf16[512,1024]{1,0:T(8,128)(2,1)} %collective-permute-done.25), channel_id=1, source_target_pairs={{8,0},{16,8},{24,16},{28,24},{20,28},{12,20},{4,12},{0,4},{9,1},{1... | collective-permute-start | bytes 3145736 | tf_op jit(solution)/shard_map/ppermute | solution.py:99
  307.2 79.6 %copy-start.66 = (bf16[512,512]{1,0:T(8,128)(2,1)}, bf16[512,512]{1,0:T(8,128)(2,1)S(1)}, u32[]{:S(2)}) copy-start(bf16[512,512]{1,0:T(8,128)(2,1)S(1)} %get-tuple-element.80) | copy-start | bytes 1572868
  320.6 85.9 %collective-permute-start.18 = (bf16[512,1024]{1,0:T(8,128)(2,1)S(1)}, bf16[512,1024]{1,0:T(8,128)(2,1)S(1)}, u32[]{:S(2)}, u32[]{:S(2)}) collective-permute-start(bf16[512,1024]{1,0:T(8,128)(2,1)S(1)} %copy-done.71), channel_id=1, source_target_pairs={{0,8},{8,16},{16,24},{24,28},{28,20},{20,12},{12,4},{4,0},{1,9},{9... | collective-permute-start | bytes 3145736 | tf_op jit(solution)/shard_map/ppermute | solution.py:98
  336.5 51.7 %collective-permute-start.21 = (bf16[512,1024]{1,0:T(8,128)(2,1)}, bf16[512,1024]{1,0:T(8,128)(2,1)S(1)}, u32[]{:S(2)}, u32[]{:S(2)}) collective-permute-start(bf16[512,1024]{1,0:T(8,128)(2,1)} %collective-permute-done.19), channel_id=1, source_target_pairs={{8,0},{16,8},{24,16},{28,24},{20,28},{12,20},{4,12},{0,4},{9,1},{1... | collective-permute-start | bytes 3145736 | tf_op jit(solution)/shard_map/ppermute | solution.py:99
  358.9 48.9 %collective-permute-start.26 = (bf16[512,1024]{1,0:T(8,128)(2,1)S(1)}, bf16[512,1024]{1,0:T(8,128)(2,1)S(1)}, u32[]{:S(2)}, u32[]{:S(2)}) collective-permute-start(bf16[512,1024]{1,0:T(8,128)(2,1)S(1)} %copy-done.74), channel_id=1, source_target_pairs={{0,8},{8,16},{16,24},{24,28},{28,20},{20,12},{12,4},{4,0},{1,9},{9... | collective-permute-start | bytes 3145736 | tf_op jit(solution)/shard_map/ppermute | solution.py:98
  378.3 26.4 %collective-permute-start.29 = (bf16[512,1024]{1,0:T(8,128)(2,1)}, bf16[512,1024]{1,0:T(8,128)(2,1)S(1)}, u32[]{:S(2)}, u32[]{:S(2)}) collective-permute-start(bf16[512,1024]{1,0:T(8,128)(2,1)} %collective-permute-done.27), channel_id=1, source_target_pairs={{8,0},{16,8},{24,16},{28,24},{20,28},{12,20},{4,12},{0,4},{9,1},{1... | collective-permute-start | bytes 3145736 | tf_op jit(solution)/shard_map/ppermute | solution.py:99
  388.2 27.9 %collective-permute-start.23 = (bf16[512,512]{1,0:T(8,128)(2,1)S(1)}, bf16[512,512]{1,0:T(8,128)(2,1)S(1)}, u32[]{:S(2)}, u32[]{:S(2)}) collective-permute-start(bf16[512,512]{1,0:T(8,128)(2,1)S(1)} %slice.809), channel_id=1, source_target_pairs={{8,0},{16,8},{24,16},{28,24},{20,28},{12,20},{4,12},{0,4},{9,1},{1... | collective-permute-start | bytes 1572872 | tf_op jit(solution)/shard_map/ppermute | solution.py:102
  404.7 16.3 %collective-permute-start.31 = (bf16[512,512]{1,0:T(8,128)(2,1)S(1)}, bf16[512,512]{1,0:T(8,128)(2,1)S(1)}, u32[]{:S(2)}, u32[]{:S(2)}) collective-permute-start(bf16[512,512]{1,0:T(8,128)(2,1)S(1)} %slice.822), channel_id=1, source_target_pairs={{8,0},{16,8},{24,16},{28,24},{20,28},{12,20},{4,12},{0,4},{9,1},{1... | collective-permute-start | bytes 1572872 | tf_op jit(solution)/shard_map/ppermute | solution.py:102
  406.6 26.2 %collective-permute-start.20 = (bf16[512,1024]{1,0:T(8,128)(2,1)S(1)}, bf16[512,1024]{1,0:T(8,128)(2,1)S(1)}, u32[]{:S(2)}, u32[]{:S(2)}) collective-permute-start(bf16[512,1024]{1,0:T(8,128)(2,1)S(1)} %collective-permute-done.18), channel_id=1, source_target_pairs={{0,8},{8,16},{16,24},{24,28},{28,20},{20,12},{12,4},{4,0},{1,9},{9... | collective-permute-start | bytes 3145736 | tf_op jit(solution)/shard_map/ppermute | solution.py:98
  408.5 44.0 %collective-permute-start.28 = (bf16[512,1024]{1,0:T(8,128)(2,1)S(1)}, bf16[512,1024]{1,0:T(8,128)(2,1)S(1)}, u32[]{:S(2)}, u32[]{:S(2)}) collective-permute-start(bf16[512,1024]{1,0:T(8,128)(2,1)S(1)} %collective-permute-done.26), channel_id=1, source_target_pairs={{0,8},{8,16},{16,24},{24,28},{28,20},{20,12},{12,4},{4,0},{1,9},{9... | collective-permute-start | bytes 3145736 | tf_op jit(solution)/shard_map/ppermute | solution.py:98
  432.8 25.3 %collective-permute-start.22 = (bf16[512,512]{1,0:T(8,128)(2,1)S(1)}, bf16[512,512]{1,0:T(8,128)(2,1)S(1)}, u32[]{:S(2)}, u32[]{:S(2)}) collective-permute-start(bf16[512,512]{1,0:T(8,128)(2,1)S(1)} %slice.808), channel_id=1, source_target_pairs={{0,8},{8,16},{16,24},{24,28},{28,20},{20,12},{12,4},{4,0},{1,9},{9... | collective-permute-start | bytes 1572872 | tf_op jit(solution)/shard_map/ppermute | solution.py:101
  452.6 11.2 %collective-permute-start.30 = (bf16[512,512]{1,0:T(8,128)(2,1)S(1)}, bf16[512,512]{1,0:T(8,128)(2,1)S(1)}, u32[]{:S(2)}, u32[]{:S(2)}) collective-permute-start(bf16[512,512]{1,0:T(8,128)(2,1)S(1)} %slice.821), channel_id=1, source_target_pairs={{0,8},{8,16},{16,24},{24,28},{28,20},{20,12},{12,4},{4,0},{1,9},{9... | collective-permute-start | bytes 1572872 | tf_op jit(solution)/shard_map/ppermute | solution.py:101
  470.3 336.0 %all-reduce.3.cloned.1.call-start = ((), (), s32[]{:S(2)}) async-start(), calls=%async_computation.2 | async-start | bytes 1179648 | tf_op jit(solution)/shard_map/psum | solution.py:222
  584.7 35.1 %collective-permute-start.48 = (bf16[2,128,512]{2,1,0:T(8,128)(2,1)S(1)}, bf16[2,128,512]{2,1,0:T(8,128)(2,1)}, u32[]{:S(2)}, u32[]{:S(2)}) collective-permute-start(bf16[2,128,512]{2,1,0:T(8,128)(2,1)S(1)} %dynamic-slice_bitcast_fusion.7), channel_id=1, source_target_pairs={{0,1},{1,0},{2,3},{3,2},{4,5},{5,4},{6,7},{7,6},{8,9},{9,8},{10,11... | collective-permute-start | bytes 786440 | tf_op jit(solution)/shard_map/ppermute | solution.py:181
  587.8 33.3 %collective-permute-start.46 = (bf16[2,128,512]{2,1,0:T(8,128)(2,1)}, bf16[2,128,512]{2,1,0:T(8,128)(2,1)}, u32[]{:S(2)}, u32[]{:S(2)}) collective-permute-start(bf16[2,128,512]{2,1,0:T(8,128)(2,1)} %dynamic-slice_bitcast_fusion.8), channel_id=1, source_target_pairs={{0,1},{1,0},{2,3},{3,2},{4,5},{5,4},{6,7},{7,6},{8,9},{9,8},{10,11... | collective-permute-start | bytes 786440 | tf_op jit(solution)/shard_map/ppermute | solution.py:181
  591.0 31.5 %collective-permute-start.44 = (bf16[2,128,1024]{2,1,0:T(8,128)(2,1)S(1)}, bf16[2,128,1024]{2,1,0:T(8,128)(2,1)S(1)}, u32[]{:S(2)}, u32[]{:S(2)}) collective-permute-start(bf16[2,128,1024]{2,1,0:T(8,128)(2,1)S(1)} %dynamic-slice_bitcast_fusion), channel_id=1, source_target_pairs={{0,1},{1,0},{2,3},{3,2},{4,5},{5,4},{6,7},{7,6},{8,9},{9,8},{10,11... | collective-permute-start | bytes 1572872 | tf_op jit(solution)/shard_map/ppermute | solution.py:181
  594.7 28.4 %collective-permute-start.42 = (bf16[2,128,1024]{2,1,0:T(8,128)(2,1)S(1)}, bf16[2,128,1024]{2,1,0:T(8,128)(2,1)S(1)}, u32[]{:S(2)}, u32[]{:S(2)}) collective-permute-start(bf16[2,128,1024]{2,1,0:T(8,128)(2,1)S(1)} %dynamic-slice_bitcast_fusion.1), channel_id=1, source_target_pairs={{0,1},{1,0},{2,3},{3,2},{4,5},{5,4},{6,7},{7,6},{8,9},{9,8},{10,11... | collective-permute-start | bytes 1572872 | tf_op jit(solution)/shard_map/ppermute | solution.py:181
  601.5 22.1 %collective-permute-start.40 = (bf16[2,128,1024]{2,1,0:T(8,128)(2,1)}, bf16[2,128,1024]{2,1,0:T(8,128)(2,1)S(1)}, u32[]{:S(2)}, u32[]{:S(2)}) collective-permute-start(bf16[2,128,1024]{2,1,0:T(8,128)(2,1)} %dynamic-slice_bitcast_fusion.2), channel_id=1, source_target_pairs={{0,1},{1,0},{2,3},{3,2},{4,5},{5,4},{6,7},{7,6},{8,9},{9,8},{10,11... | collective-permute-start | bytes 1572872 | tf_op jit(solution)/shard_map/ppermute | solution.py:181
  619.8 8.3 %collective-permute-start.38 = (bf16[2,128,1024]{2,1,0:T(8,128)(2,1)S(1)}, bf16[2,128,1024]{2,1,0:T(8,128)(2,1)S(1)}, u32[]{:S(2)}, u32[]{:S(2)}) collective-permute-start(bf16[2,128,1024]{2,1,0:T(8,128)(2,1)S(1)} %dynamic-slice_bitcast_fusion.3), channel_id=1, source_target_pairs={{0,1},{1,0},{2,3},{3,2},{4,5},{5,4},{6,7},{7,6},{8,9},{9,8},{10,11... | collective-permute-start | bytes 1572872 | tf_op jit(solution)/shard_map/ppermute | solution.py:181
  621.1 7.8 collective-permute-start.36
  622.5 2.9 collective-permute-start.34
  623.1 3.2 collective-permute-start.32
  623.7 50.1 %collective-permute-start.49 = (bf16[1,128,512]{2,1,0:T(8,128)(2,1)S(1)}, bf16[1,128,512]{2,1,0:T(8,128)(2,1)S(1)}, u32[]{:S(2)}, u32[]{:S(2)}) collective-permute-start(bf16[1,128,512]{2,1,0:T(8,128)(2,1)S(1)} %constant_dynamic-slice_fusion), channel_id=1, source_target_pairs={{0,2},{1,3},{2,0},{3,1},{4,6},{5,7},{6,4},{7,5},{8,10},{9,11},{10,... | collective-permute-start | bytes 393224 | tf_op jit(solution)/shard_map/ppermute | solution.py:181
  625.4 48.3 %collective-permute-start.47 = (bf16[1,128,512]{2,1,0:T(8,128)(2,1)S(1)}, bf16[1,128,512]{2,1,0:T(8,128)(2,1)S(1)}, u32[]{:S(2)}, u32[]{:S(2)}) collective-permute-start(bf16[1,128,512]{2,1,0:T(8,128)(2,1)S(1)} %constant_dynamic-slice_fusion.1), channel_id=1, source_target_pairs={{0,2},{1,3},{2,0},{3,1},{4,6},{5,7},{6,4},{7,5},{8,10},{9,11},{10,... | collective-permute-start | bytes 393224 | tf_op jit(solution)/shard_map/ppermute | solution.py:181
  626.3 47.4 %collective-permute-start.45 = (bf16[1,128,1024]{2,1,0:T(8,128)(2,1)S(1)}, bf16[1,128,1024]{2,1,0:T(8,128)(2,1)S(1)}, u32[]{:S(2)}, u32[]{:S(2)}) collective-permute-start(bf16[1,128,1024]{2,1,0:T(8,128)(2,1)S(1)} %constant_dynamic-slice_fusion.2), channel_id=1, source_target_pairs={{0,2},{1,3},{2,0},{3,1},{4,6},{5,7},{6,4},{7,5},{8,10},{9,11},{10,... | collective-permute-start | bytes 786440 | tf_op jit(solution)/shard_map/ppermute | solution.py:181
  628.1 22.6 %collective-permute-start.35 = (bf16[1,128,1024]{2,1,0:T(8,128)(2,1)S(1)}, bf16[1,128,1024]{2,1,0:T(8,128)(2,1)S(1)}, u32[]{:S(2)}, u32[]{:S(2)}) collective-permute-start(bf16[1,128,1024]{2,1,0:T(8,128)(2,1)S(1)} %constant_dynamic-slice_fusion.7), channel_id=1, source_target_pairs={{0,2},{1,3},{2,0},{3,1},{4,6},{5,7},{6,4},{7,5},{8,10},{9,11},{10,... | collective-permute-start | bytes 786440 | tf_op jit(solution)/shard_map/ppermute | solution.py:181
  629.0 20.0 %collective-permute-start.33 = (bf16[1,128,1024]{2,1,0:T(8,128)(2,1)S(1)}, bf16[1,128,1024]{2,1,0:T(8,128)(2,1)S(1)}, u32[]{:S(2)}, u32[]{:S(2)}) collective-permute-start(bf16[1,128,1024]{2,1,0:T(8,128)(2,1)S(1)} %constant_dynamic-slice_fusion.8), channel_id=1, source_target_pairs={{0,2},{1,3},{2,0},{3,1},{4,6},{5,7},{6,4},{7,5},{8,10},{9,11},{10,... | collective-permute-start | bytes 786440 | tf_op jit(solution)/shard_map/ppermute | solution.py:181
  649.0 9.2 %collective-permute-start.37 = (bf16[1,128,1024]{2,1,0:T(8,128)(2,1)S(1)}, bf16[1,128,1024]{2,1,0:T(8,128)(2,1)S(1)}, u32[]{:S(2)}, u32[]{:S(2)}) collective-permute-start(bf16[1,128,1024]{2,1,0:T(8,128)(2,1)S(1)} %constant_dynamic-slice_fusion.6), channel_id=1, source_target_pairs={{0,2},{1,3},{2,0},{3,1},{4,6},{5,7},{6,4},{7,5},{8,10},{9,11},{10,... | collective-permute-start | bytes 786440 | tf_op jit(solution)/shard_map/ppermute | solution.py:181
  650.8 13.1 %collective-permute-start.39 = (bf16[1,128,1024]{2,1,0:T(8,128)(2,1)S(1)}, bf16[1,128,1024]{2,1,0:T(8,128)(2,1)S(1)}, u32[]{:S(2)}, u32[]{:S(2)}) collective-permute-start(bf16[1,128,1024]{2,1,0:T(8,128)(2,1)S(1)} %constant_dynamic-slice_fusion.5), channel_id=1, source_target_pairs={{0,2},{1,3},{2,0},{3,1},{4,6},{5,7},{6,4},{7,5},{8,10},{9,11},{10,... | collective-permute-start | bytes 786440 | tf_op jit(solution)/shard_map/ppermute | solution.py:181
  658.3 11.2 %collective-permute-start.41 = (bf16[1,128,1024]{2,1,0:T(8,128)(2,1)S(1)}, bf16[1,128,1024]{2,1,0:T(8,128)(2,1)S(1)}, u32[]{:S(2)}, u32[]{:S(2)}) collective-permute-start(bf16[1,128,1024]{2,1,0:T(8,128)(2,1)S(1)} %constant_dynamic-slice_fusion.4), channel_id=1, source_target_pairs={{0,2},{1,3},{2,0},{3,1},{4,6},{5,7},{6,4},{7,5},{8,10},{9,11},{10,... | collective-permute-start | bytes 786440 | tf_op jit(solution)/shard_map/ppermute | solution.py:181
  663.9 9.6 %collective-permute-start.43 = (bf16[1,128,1024]{2,1,0:T(8,128)(2,1)S(1)}, bf16[1,128,1024]{2,1,0:T(8,128)(2,1)S(1)}, u32[]{:S(2)}, u32[]{:S(2)}) collective-permute-start(bf16[1,128,1024]{2,1,0:T(8,128)(2,1)S(1)} %constant_dynamic-slice_fusion.3), channel_id=1, source_target_pairs={{0,2},{1,3},{2,0},{3,1},{4,6},{5,7},{6,4},{7,5},{8,10},{9,11},{10,... | collective-permute-start | bytes 786440 | tf_op jit(solution)/shard_map/ppermute | solution.py:181
  (221 other events, 1639.4 us)
Sparse Core Ops, SparseCore 0:
  19.2 104.8 all-gather.5
  470.4 73.4 all-gather.7
  735.0 71.3 all-reduce.2
